TPU v7x, 512 devices: a whole 4x8x8 slice. The times are simulated.
512 devices in a mesh: row: 32 (over x, y), col: 16 (over z, core).
Axes of the slice: x: 4, y: 8, z: 8, core: 2. Of those that a mesh axis runs over, the one named last changes fastest.
Arguments:
- eigvecs: float32 [65536, 2048], P('row', 'col'), may hold values from -6 to 6
- reflectors: float32 [16, 1024, 64], P('col', 'row'), may hold values from -5 to 5, as said below
Outputs:
- transformed: float32 [65536, 2048], P('row', 'col')
Inputs may be any that keep to these rules, and one draw needn't show every extreme that they name: `reflectors`: entry 0 of every vector is 1; in sweep j, block k, entry i is 0 wherever j + k * 64 + i >= 65536.
All inputs are finite; a program needn't handle non-finite values.
Results may differ from a plain program's by a relative error of at most 0.00016.
Values sent between devices are 32-bit elements; how exact they have to be, the bound alone decides.
No kernel may reach another device: no remote copies, remote signals or barrier semaphores. Data moves between devices by JAX's collectives and lax.ppermute only.
A program may use at most 64 MiB of HBM per device.

v0:
```python
import jax
import jax.numpy as jnp
from jax import lax
from jax.sharding import PartitionSpec as P


def from_root(value, axis, root):
    mine = lax.axis_index(axis) == root
    return lax.psum(jnp.where(mine, value, jnp.zeros_like(value)), axis)


def passed_along(block, axis, distance):
    devices = range(lax.axis_size(axis))
    route = [(i - distance, i) for i in devices if i - distance in devices]
    return lax.ppermute(block, axis, route)


def apply_blocks(vectors, segment):
    leading = jnp.where(
        lax.broadcasted_iota(jnp.int32, vectors.shape, 1) == 0, jnp.ones_like(vectors), vectors
    )
    scales = 2.0 / jnp.sum(leading * leading, axis=1)
    projected = jnp.einsum("kb,kbc->kc", leading, segment, precision=lax.Precision.HIGHEST)
    return segment - (leading * scales[:, None])[:, :, None] * projected[:, None, :]


def local(eigvecs, reflectors):
    rows_dev, cols_dev = eigvecs.shape
    local_sweeps, blocks, band = reflectors.shape
    sweeps = local_sweeps * lax.axis_size("col")

    def fetch(sweep_at):
        mine = lax.dynamic_index_in_dim(reflectors, sweep_at % local_sweeps, 0, keepdims=False)
        return from_root(mine, "col", sweep_at // local_sweeps)

    position = lax.broadcasted_iota(jnp.int32, (sweeps, cols_dev), 0)
    has_lower = lax.axis_index("row") > 0

    def edge_sweep(turn, current):
        sweep_at = (sweeps - 1 - turn).astype(jnp.int32)
        vectors = fetch(sweep_at)
        upper = passed_along(current[:sweeps], "row", -1)
        extended = jnp.concatenate([current, upper], axis=0)
        segment = lax.dynamic_slice_in_dim(extended, sweep_at, rows_dev, 0).reshape(
            blocks, band, cols_dev
        )
        segment = apply_blocks(vectors, segment)
        extended = lax.dynamic_update_slice_in_dim(
            extended, segment.reshape(rows_dev, cols_dev), sweep_at, 0
        )
        returned = passed_along(extended[rows_dev:], "row", 1)
        taken = jnp.logical_and(position < sweep_at, has_lower)
        leading_rows = jnp.where(taken, returned, extended[:sweeps])
        return lax.dynamic_update_slice_in_dim(extended[:rows_dev], leading_rows, 0, 0)

    return lax.fori_loop(0, sweeps, edge_sweep, eigvecs)


def solution(mesh):
    return jax.shard_map(
        local,
        mesh=mesh,
        in_specs=(P("row", "col"), P("col", "row", None)),
        out_specs=P("row", "col"),
        check_vma=False,
    )
```

profile of v0, /device:TPU:6, one launch (start us, length us, event | category | flops | bytes accessed | tf_op | source)
XLA Modules:
  0.0 991.7 jit_solution(11961006538173376339)
XLA Ops:
  1.2 989.4 %while.16 = (s32[]{:T(128)}, f32[2048,128]{1,0:T(8,128)S(1)}, f32[1,32,64]{2,1,0:T(8,128)S(1)}, pred[]{:T(512)}, s32[]{:T(128)}, /*index=5*/u32[]{:T(128)}, s32[]{:T(128)}, s32[]{:T(128)}, s32[]{:T(128)}) while((s32[]{:T(128)}, f32[2048,128]{1,0:T(8,128)S(1)}, f32[1,32,64]{2,1,0:T(8,128)S(1)}, pred[]{:T(512)}, s32[]{:T(128)}, ...), condition=%wide.region_3.4_spmd.clone, body=%wide.region_0.3_spmd.clone.sunk | while | flops 3688521 | bytes 11805578 | solution.py:56
  1.2 5.6 collective-permute-start
  7.0 53.8 %psum.16 = f32[32,64]{1,0:T(8,128)S(1)} all-reduce(f32[32,64]{1,0:T(8,128)S(1)} %select_bitcast_fusion.2), channel_id=1, replica_groups=mesh['row'=32,'col'=16] {'col'}, use_global_device_ids=true, to_apply=%region_1.1 | all-reduce | flops 2048 | bytes 16384 | tf_op jit(solution)/shard_map/while/body/eval_jaxpr/psum | solution.py:9
  62.5 4.0 dynamic_update_slice.26
  68.5 5.6 collective-permute-done.1
  76.2 45.7 %psum.16 = f32[32,64]{1,0:T(8,128)S(1)} all-reduce(f32[32,64]{1,0:T(8,128)S(1)} %select_bitcast_fusion.2), channel_id=1, replica_groups=mesh['row'=32,'col'=16] {'col'}, use_global_device_ids=true, to_apply=%region_1.1 | all-reduce | flops 2048 | bytes 16384 | tf_op jit(solution)/shard_map/while/body/eval_jaxpr/psum | solution.py:9
  123.6 4.0 dynamic_update_slice.26
  127.6 3.9 collective-permute-start.1
  131.6 3.6 collective-permute-done.1
  137.3 45.7 %psum.16 = f32[32,64]{1,0:T(8,128)S(1)} all-reduce(f32[32,64]{1,0:T(8,128)S(1)} %select_bitcast_fusion.2), channel_id=1, replica_groups=mesh['row'=32,'col'=16] {'col'}, use_global_device_ids=true, to_apply=%region_1.1 | all-reduce | flops 2048 | bytes 16384 | tf_op jit(solution)/shard_map/while/body/eval_jaxpr/psum | solution.py:9
  184.7 4.0 dynamic_update_slice.26
  188.7 3.9 collective-permute-start.1
  192.7 3.6 collective-permute-done.1
  198.4 45.7 %psum.16 = f32[32,64]{1,0:T(8,128)S(1)} all-reduce(f32[32,64]{1,0:T(8,128)S(1)} %select_bitcast_fusion.2), channel_id=1, replica_groups=mesh['row'=32,'col'=16] {'col'}, use_global_device_ids=true, to_apply=%region_1.1 | all-reduce | flops 2048 | bytes 16384 | tf_op jit(solution)/shard_map/while/body/eval_jaxpr/psum | solution.py:9
  245.8 4.0 dynamic_update_slice.26
  249.8 3.9 collective-permute-start.1
  253.8 3.6 collective-permute-done.1
  259.5 45.7 %psum.16 = f32[32,64]{1,0:T(8,128)S(1)} all-reduce(f32[32,64]{1,0:T(8,128)S(1)} %select_bitcast_fusion.2), channel_id=1, replica_groups=mesh['row'=32,'col'=16] {'col'}, use_global_device_ids=true, to_apply=%region_1.1 | all-reduce | flops 2048 | bytes 16384 | tf_op jit(solution)/shard_map/while/body/eval_jaxpr/psum | solution.py:9
  306.9 4.0 dynamic_update_slice.26
  310.9 3.9 collective-permute-start.1
  314.9 3.6 collective-permute-done.1
  320.6 45.7 %psum.16 = f32[32,64]{1,0:T(8,128)S(1)} all-reduce(f32[32,64]{1,0:T(8,128)S(1)} %select_bitcast_fusion.2), channel_id=1, replica_groups=mesh['row'=32,'col'=16] {'col'}, use_global_device_ids=true, to_apply=%region_1.1 | all-reduce | flops 2048 | bytes 16384 | tf_op jit(solution)/shard_map/while/body/eval_jaxpr/psum | solution.py:9
  368.0 4.0 dynamic_update_slice.26
  372.0 3.9 collective-permute-start.1
  376.0 3.6 collective-permute-done.1
  381.7 45.7 %psum.16 = f32[32,64]{1,0:T(8,128)S(1)} all-reduce(f32[32,64]{1,0:T(8,128)S(1)} %select_bitcast_fusion.2), channel_id=1, replica_groups=mesh['row'=32,'col'=16] {'col'}, use_global_device_ids=true, to_apply=%region_1.1 | all-reduce | flops 2048 | bytes 16384 | tf_op jit(solution)/shard_map/while/body/eval_jaxpr/psum | solution.py:9
  429.1 4.0 dynamic_update_slice.26
  433.1 3.9 collective-permute-start.1
  437.1 3.6 collective-permute-done.1
  442.8 45.7 %psum.16 = f32[32,64]{1,0:T(8,128)S(1)} all-reduce(f32[32,64]{1,0:T(8,128)S(1)} %select_bitcast_fusion.2), channel_id=1, replica_groups=mesh['row'=32,'col'=16] {'col'}, use_global_device_ids=true, to_apply=%region_1.1 | all-reduce | flops 2048 | bytes 16384 | tf_op jit(solution)/shard_map/while/body/eval_jaxpr/psum | solution.py:9
  490.2 3.9 dynamic_update_slice.26
  494.2 3.9 collective-permute-start.1
  498.2 3.6 collective-permute-done.1
  503.9 45.7 %psum.16 = f32[32,64]{1,0:T(8,128)S(1)} all-reduce(f32[32,64]{1,0:T(8,128)S(1)} %select_bitcast_fusion.2), channel_id=1, replica_groups=mesh['row'=32,'col'=16] {'col'}, use_global_device_ids=true, to_apply=%region_1.1 | all-reduce | flops 2048 | bytes 16384 | tf_op jit(solution)/shard_map/while/body/eval_jaxpr/psum | solution.py:9
  551.3 4.0 dynamic_update_slice.26
  555.3 3.9 collective-permute-start.1
  559.3 3.6 collective-permute-done.1
  565.0 45.7 %psum.16 = f32[32,64]{1,0:T(8,128)S(1)} all-reduce(f32[32,64]{1,0:T(8,128)S(1)} %select_bitcast_fusion.2), channel_id=1, replica_groups=mesh['row'=32,'col'=16] {'col'}, use_global_device_ids=true, to_apply=%region_1.1 | all-reduce | flops 2048 | bytes 16384 | tf_op jit(solution)/shard_map/while/body/eval_jaxpr/psum | solution.py:9
  612.4 4.0 dynamic_update_slice.26
  616.4 3.9 collective-permute-start.1
  620.4 3.6 collective-permute-done.1
  626.1 45.7 %psum.16 = f32[32,64]{1,0:T(8,128)S(1)} all-reduce(f32[32,64]{1,0:T(8,128)S(1)} %select_bitcast_fusion.2), channel_id=1, replica_groups=mesh['row'=32,'col'=16] {'col'}, use_global_device_ids=true, to_apply=%region_1.1 | all-reduce | flops 2048 | bytes 16384 | tf_op jit(solution)/shard_map/while/body/eval_jaxpr/psum | solution.py:9
  673.5 4.0 dynamic_update_slice.26
  677.5 3.9 collective-permute-start.1
  681.5 3.6 collective-permute-done.1
  687.2 45.7 %psum.16 = f32[32,64]{1,0:T(8,128)S(1)} all-reduce(f32[32,64]{1,0:T(8,128)S(1)} %select_bitcast_fusion.2), channel_id=1, replica_groups=mesh['row'=32,'col'=16] {'col'}, use_global_device_ids=true, to_apply=%region_1.1 | all-reduce | flops 2048 | bytes 16384 | tf_op jit(solution)/shard_map/while/body/eval_jaxpr/psum | solution.py:9
  734.6 4.0 dynamic_update_slice.26
  738.6 3.9 collective-permute-start.1
  742.6 3.6 collective-permute-done.1
  748.3 45.7 %psum.16 = f32[32,64]{1,0:T(8,128)S(1)} all-reduce(f32[32,64]{1,0:T(8,128)S(1)} %select_bitcast_fusion.2), channel_id=1, replica_groups=mesh['row'=32,'col'=16] {'col'}, use_global_device_ids=true, to_apply=%region_1.1 | all-reduce | flops 2048 | bytes 16384 | tf_op jit(solution)/shard_map/while/body/eval_jaxpr/psum | solution.py:9
  795.7 4.0 dynamic_update_slice.26
  799.7 3.9 collective-permute-start.1
  803.7 3.6 collective-permute-done.1
  809.4 45.7 %psum.16 = f32[32,64]{1,0:T(8,128)S(1)} all-reduce(f32[32,64]{1,0:T(8,128)S(1)} %select_bitcast_fusion.2), channel_id=1, replica_groups=mesh['row'=32,'col'=16] {'col'}, use_global_device_ids=true, to_apply=%region_1.1 | all-reduce | flops 2048 | bytes 16384 | tf_op jit(solution)/shard_map/while/body/eval_jaxpr/psum | solution.py:9
  856.8 4.0 dynamic_update_slice.26
  860.8 3.9 collective-permute-start.1
  864.8 3.6 collective-permute-done.1
  870.5 45.7 %psum.16 = f32[32,64]{1,0:T(8,128)S(1)} all-reduce(f32[32,64]{1,0:T(8,128)S(1)} %select_bitcast_fusion.2), channel_id=1, replica_groups=mesh['row'=32,'col'=16] {'col'}, use_global_device_ids=true, to_apply=%region_1.1 | all-reduce | flops 2048 | bytes 16384 | tf_op jit(solution)/shard_map/while/body/eval_jaxpr/psum | solution.py:9
  917.9 4.0 dynamic_update_slice.26
  921.9 3.9 collective-permute-start.1
  925.9 3.6 collective-permute-done.1
  931.6 45.7 %psum.16 = f32[32,64]{1,0:T(8,128)S(1)} all-reduce(f32[32,64]{1,0:T(8,128)S(1)} %select_bitcast_fusion.2), channel_id=1, replica_groups=mesh['row'=32,'col'=16] {'col'}, use_global_device_ids=true, to_apply=%region_1.1 | all-reduce | flops 2048 | bytes 16384 | tf_op jit(solution)/shard_map/while/body/eval_jaxpr/psum | solution.py:9
  979.0 4.0 dynamic_update_slice.26
  983.0 3.9 collective-permute-start.1
  (279 shorter events, 66.2 us)
Async XLA Ops:
  0.0 0.7 copy-start.2
  0.0 1.2 copy-start.1
  1.2 59.8 %collective-permute-start = (f32[16,128]{1,0:T(8,128)S(1)}, f32[16,128]{1,0:T(8,128)S(1)}, u32[]{:S(2)}, u32[]{:S(2)}) collective-permute-start(f32[16,128]{1,0:T(8,128)S(1)} %slice.55), channel_id=1, source_target_pairs={{16,0},{32,16},{48,32},{64,48},{80,64},{96,80},{112,96},{128,112},... | collective-permute-start | bytes 24584 | tf_op jit(solution)/shard_map/while/body/eval_jaxpr/ppermute | solution.py:15
  66.5 7.7 collective-permute-start.1
  74.1 48.0 %collective-permute-start = (f32[16,128]{1,0:T(8,128)S(1)}, f32[16,128]{1,0:T(8,128)S(1)}, u32[]{:S(2)}, u32[]{:S(2)}) collective-permute-start(f32[16,128]{1,0:T(8,128)S(1)} %slice.55), channel_id=1, source_target_pairs={{16,0},{32,16},{48,32},{64,48},{80,64},{96,80},{112,96},{128,112},... | collective-permute-start | bytes 24584 | tf_op jit(solution)/shard_map/while/body/eval_jaxpr/ppermute | solution.py:15
  127.6 7.7 collective-permute-start.1
  135.2 48.0 %collective-permute-start = (f32[16,128]{1,0:T(8,128)S(1)}, f32[16,128]{1,0:T(8,128)S(1)}, u32[]{:S(2)}, u32[]{:S(2)}) collective-permute-start(f32[16,128]{1,0:T(8,128)S(1)} %slice.55), channel_id=1, source_target_pairs={{16,0},{32,16},{48,32},{64,48},{80,64},{96,80},{112,96},{128,112},... | collective-permute-start | bytes 24584 | tf_op jit(solution)/shard_map/while/body/eval_jaxpr/ppermute | solution.py:15
  188.7 7.7 collective-permute-start.1
  196.3 48.0 %collective-permute-start = (f32[16,128]{1,0:T(8,128)S(1)}, f32[16,128]{1,0:T(8,128)S(1)}, u32[]{:S(2)}, u32[]{:S(2)}) collective-permute-start(f32[16,128]{1,0:T(8,128)S(1)} %slice.55), channel_id=1, source_target_pairs={{16,0},{32,16},{48,32},{64,48},{80,64},{96,80},{112,96},{128,112},... | collective-permute-start | bytes 24584 | tf_op jit(solution)/shard_map/while/body/eval_jaxpr/ppermute | solution.py:15
  249.8 7.7 collective-permute-start.1
  257.4 48.0 %collective-permute-start = (f32[16,128]{1,0:T(8,128)S(1)}, f32[16,128]{1,0:T(8,128)S(1)}, u32[]{:S(2)}, u32[]{:S(2)}) collective-permute-start(f32[16,128]{1,0:T(8,128)S(1)} %slice.55), channel_id=1, source_target_pairs={{16,0},{32,16},{48,32},{64,48},{80,64},{96,80},{112,96},{128,112},... | collective-permute-start | bytes 24584 | tf_op jit(solution)/shard_map/while/body/eval_jaxpr/ppermute | solution.py:15
  310.9 7.7 collective-permute-start.1
  318.5 48.0 %collective-permute-start = (f32[16,128]{1,0:T(8,128)S(1)}, f32[16,128]{1,0:T(8,128)S(1)}, u32[]{:S(2)}, u32[]{:S(2)}) collective-permute-start(f32[16,128]{1,0:T(8,128)S(1)} %slice.55), channel_id=1, source_target_pairs={{16,0},{32,16},{48,32},{64,48},{80,64},{96,80},{112,96},{128,112},... | collective-permute-start | bytes 24584 | tf_op jit(solution)/shard_map/while/body/eval_jaxpr/ppermute | solution.py:15
  372.0 7.7 collective-permute-start.1
  379.6 48.0 %collective-permute-start = (f32[16,128]{1,0:T(8,128)S(1)}, f32[16,128]{1,0:T(8,128)S(1)}, u32[]{:S(2)}, u32[]{:S(2)}) collective-permute-start(f32[16,128]{1,0:T(8,128)S(1)} %slice.55), channel_id=1, source_target_pairs={{16,0},{32,16},{48,32},{64,48},{80,64},{96,80},{112,96},{128,112},... | collective-permute-start | bytes 24584 | tf_op jit(solution)/shard_map/while/body/eval_jaxpr/ppermute | solution.py:15
  433.1 7.7 collective-permute-start.1
  440.8 48.0 %collective-permute-start = (f32[16,128]{1,0:T(8,128)S(1)}, f32[16,128]{1,0:T(8,128)S(1)}, u32[]{:S(2)}, u32[]{:S(2)}) collective-permute-start(f32[16,128]{1,0:T(8,128)S(1)} %slice.55), channel_id=1, source_target_pairs={{16,0},{32,16},{48,32},{64,48},{80,64},{96,80},{112,96},{128,112},... | collective-permute-start | bytes 24584 | tf_op jit(solution)/shard_map/while/body/eval_jaxpr/ppermute | solution.py:15
  494.2 7.7 collective-permute-start.1
  501.8 48.0 %collective-permute-start = (f32[16,128]{1,0:T(8,128)S(1)}, f32[16,128]{1,0:T(8,128)S(1)}, u32[]{:S(2)}, u32[]{:S(2)}) collective-permute-start(f32[16,128]{1,0:T(8,128)S(1)} %slice.55), channel_id=1, source_target_pairs={{16,0},{32,16},{48,32},{64,48},{80,64},{96,80},{112,96},{128,112},... | collective-permute-start | bytes 24584 | tf_op jit(solution)/shard_map/while/body/eval_jaxpr/ppermute | solution.py:15
  555.3 7.7 collective-permute-start.1
  562.9 48.0 %collective-permute-start = (f32[16,128]{1,0:T(8,128)S(1)}, f32[16,128]{1,0:T(8,128)S(1)}, u32[]{:S(2)}, u32[]{:S(2)}) collective-permute-start(f32[16,128]{1,0:T(8,128)S(1)} %slice.55), channel_id=1, source_target_pairs={{16,0},{32,16},{48,32},{64,48},{80,64},{96,80},{112,96},{128,112},... | collective-permute-start | bytes 24584 | tf_op jit(solution)/shard_map/while/body/eval_jaxpr/ppermute | solution.py:15
  616.4 7.7 collective-permute-start.1
  624.1 48.0 %collective-permute-start = (f32[16,128]{1,0:T(8,128)S(1)}, f32[16,128]{1,0:T(8,128)S(1)}, u32[]{:S(2)}, u32[]{:S(2)}) collective-permute-start(f32[16,128]{1,0:T(8,128)S(1)} %slice.55), channel_id=1, source_target_pairs={{16,0},{32,16},{48,32},{64,48},{80,64},{96,80},{112,96},{128,112},... | collective-permute-start | bytes 24584 | tf_op jit(solution)/shard_map/while/body/eval_jaxpr/ppermute | solution.py:15
  677.5 7.7 collective-permute-start.1
  685.2 48.0 %collective-permute-start = (f32[16,128]{1,0:T(8,128)S(1)}, f32[16,128]{1,0:T(8,128)S(1)}, u32[]{:S(2)}, u32[]{:S(2)}) collective-permute-start(f32[16,128]{1,0:T(8,128)S(1)} %slice.55), channel_id=1, source_target_pairs={{16,0},{32,16},{48,32},{64,48},{80,64},{96,80},{112,96},{128,112},... | collective-permute-start | bytes 24584 | tf_op jit(solution)/shard_map/while/body/eval_jaxpr/ppermute | solution.py:15
  738.6 7.7 collective-permute-start.1
  746.3 48.0 %collective-permute-start = (f32[16,128]{1,0:T(8,128)S(1)}, f32[16,128]{1,0:T(8,128)S(1)}, u32[]{:S(2)}, u32[]{:S(2)}) collective-permute-start(f32[16,128]{1,0:T(8,128)S(1)} %slice.55), channel_id=1, source_target_pairs={{16,0},{32,16},{48,32},{64,48},{80,64},{96,80},{112,96},{128,112},... | collective-permute-start | bytes 24584 | tf_op jit(solution)/shard_map/while/body/eval_jaxpr/ppermute | solution.py:15
  799.7 7.7 collective-permute-start.1
  807.4 48.0 %collective-permute-start = (f32[16,128]{1,0:T(8,128)S(1)}, f32[16,128]{1,0:T(8,128)S(1)}, u32[]{:S(2)}, u32[]{:S(2)}) collective-permute-start(f32[16,128]{1,0:T(8,128)S(1)} %slice.55), channel_id=1, source_target_pairs={{16,0},{32,16},{48,32},{64,48},{80,64},{96,80},{112,96},{128,112},... | collective-permute-start | bytes 24584 | tf_op jit(solution)/shard_map/while/body/eval_jaxpr/ppermute | solution.py:15
  860.8 7.7 collective-permute-start.1
  868.5 48.0 %collective-permute-start = (f32[16,128]{1,0:T(8,128)S(1)}, f32[16,128]{1,0:T(8,128)S(1)}, u32[]{:S(2)}, u32[]{:S(2)}) collective-permute-start(f32[16,128]{1,0:T(8,128)S(1)} %slice.55), channel_id=1, source_target_pairs={{16,0},{32,16},{48,32},{64,48},{80,64},{96,80},{112,96},{128,112},... | collective-permute-start | bytes 24584 | tf_op jit(solution)/shard_map/while/body/eval_jaxpr/ppermute | solution.py:15
  921.9 7.7 collective-permute-start.1
  929.6 48.0 %collective-permute-start = (f32[16,128]{1,0:T(8,128)S(1)}, f32[16,128]{1,0:T(8,128)S(1)}, u32[]{:S(2)}, u32[]{:S(2)}) collective-permute-start(f32[16,128]{1,0:T(8,128)S(1)} %slice.55), channel_id=1, source_target_pairs={{16,0},{32,16},{48,32},{64,48},{80,64},{96,80},{112,96},{128,112},... | collective-permute-start | bytes 24584 | tf_op jit(solution)/shard_map/while/body/eval_jaxpr/ppermute | solution.py:15
  983.0 7.7 collective-permute-start.1
  990.7 1.0 copy-start
where the time goes:
time: 993 us; the launch traced here: 992 us
  blocking collectives  739 us (74%)
  starting transfers between devices  95.2 us (10%)
  local copies, waits for them, and re-layouts  70.9 us (7%)
  waiting for transfers between devices  60.4 us (6%)
  matrix products  15.5 us (2%)
    psum x16, blocking collectives, from_root(): return lax.psum(jnp.where(mine, value, jnp.zeros_like(value)), axis)  739 us
    ppermute x32, starting transfers between devices, passed_along(): return lax.ppermute(block, axis, route)  95.2 us
    dynamic_update_slice x16, local copies, waits for them, and re-layouts, edge_sweep(): lax.dynamic_update_slice_in_dim(extended, segment.reshape(rows_dev, cols_...  63.6 us
    ppermute x32, waiting for transfers between devices, passed_along(): return lax.ppermute(block, axis, route)  60.4 us
  transfers between devices with their start and end apart: 32, of which 16 were waited for; matrix products, arithmetic and copies ran while one was open for 1% of the time, Pallas kernels for 0%

commit v1 on v0

v1 whole, which is shorter than its diff:
```python
import functools
import jax, jax.numpy as jnp
from jax import lax
from jax.experimental import pallas as pl
from jax.experimental.pallas import tpu as pltpu

S, B = 16, 64

def bcast(tile, i, ng):
    lo = jnp.broadcast_to(tile[:, i:i+1], (16, 128))
    if ng == 2:
        return lo
    hi = jnp.broadcast_to(tile[:, 64+i:65+i], (16, 128))
    return jnp.concatenate([lo, hi], 0)

def taus(tile, ng):
    sq = tile * tile
    lo = 2.0 / jnp.sum(sq[:, :64], axis=1, keepdims=True)
    lo = jnp.broadcast_to(lo, (16, 128))
    if ng == 2:
        return lo
    hi = 2.0 / jnp.sum(sq[:, 64:], axis=1, keepdims=True)
    return jnp.concatenate([lo, jnp.broadcast_to(hi, (16, 128))], 0)

def sweep_body(j, g_ref, t_ref, ng, nacc=4):
    tile = g_ref[j]
    acc = [None] * nacc
    for i in range(B):
        p = bcast(tile, i, ng) * t_ref[j + i] if i else t_ref[j]
        a = i % nacc
        acc[a] = p if acc[a] is None else acc[a] + p
    while len(acc) > 1:
        acc = [acc[a] + acc[a+1] for a in range(0, len(acc), 2)]
    w = acc[0] * taus(tile, ng)
    for i in range(B):
        t_ref[j + i] = t_ref[j + i] - (bcast(tile, i, ng) * w if i else w)

def k_all(x_ref, g_ref, halo_ref, out_ref, ret_ref, t_ref):
    ng = 4
    def load(b, c):
        t_ref[b] = x_ref[pl.ds(b, 32, stride=64), :]
        return c
    lax.fori_loop(0, 64, load, 0, unroll=8)
    last = lax.broadcasted_iota(jnp.int32, (32, 128), 0) == 31
    for i in range(15):
        r = pltpu.roll(t_ref[i], 31, 0)
        t_ref[64 + i] = jnp.where(last, jnp.broadcast_to(halo_ref[i:i+1, :], (32, 128)), r)
    def sweep(n, c):
        j = S - 1 - n
        sweep_body(j, g_ref, t_ref, ng)
        @pl.when(j > 0)
        def _():
            e = t_ref[j + 63]
            t_ref[j - 1] = pltpu.roll(e, 1, 0)
            ret_ref[pl.ds(j - 1, 1), :] = e[31:32, :]
        return c
    lax.fori_loop(0, S, sweep, 0)
    def store(b, c):
        out_ref[pl.ds(b, 16, stride=64), :] = t_ref[b, 16:, :]
        return c
    lax.fori_loop(0, 64, store, 0, unroll=8)

def call_all(x, g, halo):
    return pl.pallas_call(
        k_all,
        out_shape=(jax.ShapeDtypeStruct((2048, 128), jnp.float32), jax.ShapeDtypeStruct((16, 128), jnp.float32)),
        grid=(1,),
        in_specs=[pl.BlockSpec((2048, 128), lambda i: (0, 0)), pl.BlockSpec((16, 16, 128), lambda i: (0, 0, 0)), pl.BlockSpec((16, 128), lambda i: (0, 0))],
        out_specs=(pl.BlockSpec((1024, 128), lambda i: (1, 0)), pl.BlockSpec((16, 128), lambda i: (0, 0))),
        scratch_shapes=[pltpu.VMEM((80, 32, 128), jnp.float32)],
        name="upper",
    )(x, g, halo)

def k_low(x_ref, g_ref, ret_ref, prev_ref, out_ref, t_ref):
    ng = 2
    def load(b, c):
        t_ref[b] = x_ref[pl.ds(b, 16, stride=64), :]
        return c
    lax.fori_loop(0, 64, load, 0, unroll=8)
    last = lax.broadcasted_iota(jnp.int32, (16, 128), 0) == 15
    first = lax.broadcasted_iota(jnp.int32, (16, 128), 0) == 0
    for i in range(15):
        r = pltpu.roll(t_ref[i], 15, 0)
        t_ref[64 + i] = jnp.where(last, jnp.broadcast_to(x_ref[1024 + i:1025 + i, :], (16, 128)), r)
    def sweep(n, c):
        j = S - 1 - n
        sweep_body(j, g_ref, t_ref, ng)
        @pl.when(j > 0)
        def _():
            t_ref[j - 1] = jnp.where(first, jnp.broadcast_to(ret_ref[pl.ds(j - 1, 1), :], (16, 128)), pltpu.roll(t_ref[j + 63], 1, 0))
        return c
    lax.fori_loop(0, S, sweep, 0)
    def store(b, c):
        out_ref[pl.ds(b, 16, stride=64), :] = t_ref[b]
        return c
    lax.fori_loop(0, 64, store, 0, unroll=8)

def call_low(x, g, ret, prev):
    return pl.pallas_call(
        k_low,
        out_shape=jax.ShapeDtypeStruct((2048, 128), jnp.float32),
        grid=(1,),
        in_specs=[pl.BlockSpec((1040, 128), lambda i: (0, 0)), pl.BlockSpec((16, 16, 128), lambda i: (0, 0, 0)), pl.BlockSpec((16, 128), lambda i: (0, 0)), pl.BlockSpec(memory_space=pl.ANY)],
        out_specs=pl.BlockSpec((1024, 128), lambda i: (0, 0)),
        scratch_shapes=[pltpu.VMEM((80, 16, 128), jnp.float32)],
        input_output_aliases={3: 0},
        name="lower",
    )(x, g, ret, prev)

from jax.sharding import PartitionSpec as P


def neighbour(value, step):
    owners = lax.axis_size("row")
    return lax.ppermute(value, "row", [(i, (i + step) % owners) for i in range(owners)])


def local(eigvecs, reflectors):
    half = reflectors.shape[1] // 2
    packed = jnp.concatenate([reflectors[:, :half], reflectors[:, half:]], axis=2)
    copies = jnp.broadcast_to(packed, (lax.axis_size("col"),) + packed.shape[1:])
    halo = neighbour(eigvecs[:16], -1)
    vectors = lax.all_to_all(copies, "col", 0, 0, tiled=True)
    upper, leaving = call_all(eigvecs, vectors, halo)
    entering = neighbour(leaving, 1)
    return call_low(eigvecs, vectors, entering, upper)


def solution(mesh):
    return jax.shard_map(
        local,
        mesh=mesh,
        in_specs=(P("row", "col"), P("col", "row", None)),
        out_specs=P("row", "col"),
        check_vma=False,
    )
```

time: 993 us -> 58.6 us (0.06)
  the two profiles are of different devices: /device:TPU:6 before, /device:TPU:1 now
where the time goes in v1:
time: 58.6 us; the launch traced here: 58.1 us
  Pallas kernels  25.9 us (44%)
  starting transfers between devices  22.1 us (38%)
  waiting for transfers between devices  6.48 us (11%)
  local copies, waits for them, and re-layouts  3.53 us (6%)
    pallas_call x1, Pallas kernels, call_all(): pl.pallas_call(k_all, out_shape=(jax.ShapeDtypeStruct((2048, 128), jnp.fl...  15.5 us
    all_to_all x1, starting transfers between devices, local(): vectors = lax.all_to_all(copies, 'col', 0, 0, tiled=True)  11.8 us
    pallas_call x1, Pallas kernels, call_low(): pl.pallas_call(k_low, out_shape=jax.ShapeDtypeStruct((2048, 128), jnp.flo...  10.4 us
    ppermute x2, starting transfers between devices, neighbour(): lax.ppermute(value, 'row', [(i, (i + step) % owners) for i in range(owner...  10.3 us
    ppermute x2, waiting for transfers between devices, neighbour(): lax.ppermute(value, 'row', [(i, (i + step) % owners) for i in range(owner...  6.09 us
    unnamed x6, local copies, waits for them, and re-layouts  1.45 us
  transfers between devices with their start and end apart: 3, of which 3 were waited for; matrix products, arithmetic and copies ran while one was open for 1% of the time, Pallas kernels for 0%

profile of v1, /device:TPU:1, one launch (start us, length us, event | category | flops | bytes accessed | tf_op | source)
XLA Modules:
  0.0 58.1 jit_solution(15316059905316559649)
XLA Ops:
  0.0 0.7 %fusion = (f32[1,16,64]{2,1,0:T(8,128)S(1)}, f32[1,16,64]{2,1,0:T(8,128)S(1)}) fusion(f32[1,32,64]{2,1,0:T(8,128)} %param.3), kind=kLoop, calls=%fused_computation.1 | loop fusion | bytes 16384 | tf_op jit(solution)/shard_map/slice | solution.py:120
  0.7 0.1 maximum_bitcast_fusion
  0.8 0.7 %broadcast_in_dim.8 = f32[16,16,128]{2,1,0:T(8,128)} broadcast(f32[16,128]{1,0:T(8,128)S(1)} %maximum_bitcast_fusion), dimensions={1,2} | broadcast | bytes 139264 | tf_op jit(solution)/shard_map/broadcast_in_dim | solution.py:121
  1.5 11.8 %all-to-all-start = ((f32[16,16,128]{2,1,0:T(8,128)}), f32[16,16,128]{2,1,0:T(8,128)S(1)}, u32[]{:S(2)}, u32[]{:S(2)}) async-start(f32[16,16,128]{2,1,0:T(8,128)} %broadcast_in_dim.8), calls=%async_computation | async-start | bytes 262144 | tf_op jit(solution)/shard_map/all_to_all | solution.py:123
  13.3 0.7 %slice.11 = f32[16,128]{1,0:T(8,128)S(1)} slice(f32[2048,128]{1,0:T(8,128)} %x_ref.3), slice={[0:16], [0:128]} | slice | bytes 16384 | tf_op jit(solution)/shard_map/slice | solution.py:122
  14.0 7.3 %collective-permute-start = (f32[16,128]{1,0:T(8,128)S(1)}, f32[16,128]{1,0:T(8,128)S(1)}, u32[]{:S(2)}, u32[]{:S(2)}) collective-permute-start(f32[16,128]{1,0:T(8,128)S(1)} %slice.11), channel_id=1, source_target_pairs={{0,496},{16,0},{32,16},{48,32},{64,48},{80,64},{96,80},{112,96},{1... | collective-permute-start | bytes 24584 | tf_op jit(solution)/shard_map/ppermute | solution.py:115
  21.3 0.8 %collective-permute-done.halo_ref = f32[16,128]{1,0:T(8,128)S(1)} collective-permute-done((f32[16,128]{1,0:T(8,128)S(1)}, f32[16,128]{1,0:T(8,128)S(1)}, u32[]{:S(2)}, u32[]{:S(2)}) %collective-permute-start) | collective-permute-done | bytes 8224 | tf_op jit(solution)/shard_map/ppermute | solution.py:115
  22.1 0.0 copy-start.1
  22.1 0.4 all-to-all-done.g_ref
  22.5 0.2 copy-done.1
  22.7 0.0 copy-start
  22.7 0.6 %copy-done = f32[16,16,128]{2,1,0:T(8,128)} copy-done((f32[16,16,128]{2,1,0:T(8,128)}, f32[16,16,128]{2,1,0:T(8,128)S(1)}, u32[]{:S(2)}) %copy-start) | copy-done | bytes 131096
  23.3 15.5 %upper.1 = (f32[2048,128]{1,0:T(8,128)}, f32[16,128]{1,0:T(8,128)}) custom-call(f32[2048,128]{1,0:T(8,128)} %x_ref.3, f32[16,16,128]{2,1,0:T(8,128)} %copy-done, f32[16,128]{1,0:T(8,128)} %copy-done.1), custom_call_target="tpu_custom_call" | custom-call | tf_op jit(solution)/shard_map/upper/pallas_call | solution.py:64
  38.8 3.0 %collective-permute-start.1 = (f32[16,128]{1,0:T(8,128)}, f32[16,128]{1,0:T(8,128)S(1)}, u32[]{:S(2)}, u32[]{:S(2)}) collective-permute-start(f32[16,128]{1,0:T(8,128)} %get-tuple-element.7), channel_id=1, source_target_pairs={{0,16},{16,32},{32,48},{48,64},{64,80},{80,96},{96,112},{112,128},... | collective-permute-start | bytes 24584 | tf_op jit(solution)/shard_map/ppermute | solution.py:115
  41.8 5.3 %collective-permute-done.1.ret_ref = f32[16,128]{1,0:T(8,128)S(1)} collective-permute-done((f32[16,128]{1,0:T(8,128)}, f32[16,128]{1,0:T(8,128)S(1)}, u32[]{:S(2)}, u32[]{:S(2)}) %collective-permute-start.1) | collective-permute-done | bytes 8224 | tf_op jit(solution)/shard_map/ppermute | solution.py:115
  47.1 0.0 copy-start.2
  47.1 0.6 %copy-done.2 = f32[16,128]{1,0:T(8,128)} copy-done((f32[16,128]{1,0:T(8,128)}, f32[16,128]{1,0:T(8,128)S(1)}, u32[]{:S(2)}) %copy-start.2) | copy-done | bytes 8216
  47.7 10.4 %lower.1 = f32[2048,128]{1,0:T(8,128)} custom-call(f32[2048,128]{1,0:T(8,128)} %x_ref.3, f32[16,16,128]{2,1,0:T(8,128)} %copy-done, f32[16,128]{1,0:T(8,128)} %copy-done.2, f32[2048,128]{1,0:T(8,128)} %get-tuple-element.8.prev_ref), custom_call_target="tpu_custom_call", output_to_operand_aliasing={{}: (3, {})} | custom-call | tf_op jit(solution)/shard_map/lower/pallas_call | solution.py:99
Async XLA Ops:
  1.5 21.0 %all-to-all-start = ((f32[16,16,128]{2,1,0:T(8,128)}), f32[16,16,128]{2,1,0:T(8,128)S(1)}, u32[]{:S(2)}, u32[]{:S(2)}) async-start(f32[16,16,128]{2,1,0:T(8,128)} %broadcast_in_dim.8), calls=%async_computation | async-start | bytes 262144 | tf_op jit(solution)/shard_map/all_to_all | solution.py:123
  14.0 8.1 %collective-permute-start = (f32[16,128]{1,0:T(8,128)S(1)}, f32[16,128]{1,0:T(8,128)S(1)}, u32[]{:S(2)}, u32[]{:S(2)}) collective-permute-start(f32[16,128]{1,0:T(8,128)S(1)} %slice.11), channel_id=1, source_target_pairs={{0,496},{16,0},{32,16},{48,32},{64,48},{80,64},{96,80},{112,96},{1... | collective-permute-start | bytes 24584 | tf_op jit(solution)/shard_map/ppermute | solution.py:115
  22.1 0.6 %copy-start.1 = (f32[16,128]{1,0:T(8,128)}, f32[16,128]{1,0:T(8,128)S(1)}, u32[]{:S(2)}) copy-start(f32[16,128]{1,0:T(8,128)S(1)} %collective-permute-done.halo_ref) | copy-start | bytes 24580
  22.7 0.6 %copy-start = (f32[16,16,128]{2,1,0:T(8,128)}, f32[16,16,128]{2,1,0:T(8,128)S(1)}, u32[]{:S(2)}) copy-start(f32[16,16,128]{2,1,0:T(8,128)S(1)} %all-to-all-done.g_ref) | copy-start | bytes 393220
  38.8 8.3 %collective-permute-start.1 = (f32[16,128]{1,0:T(8,128)}, f32[16,128]{1,0:T(8,128)S(1)}, u32[]{:S(2)}, u32[]{:S(2)}) collective-permute-start(f32[16,128]{1,0:T(8,128)} %get-tuple-element.7), channel_id=1, source_target_pairs={{0,16},{16,32},{32,48},{48,64},{64,80},{80,96},{96,112},{112,128},... | collective-permute-start | bytes 24584 | tf_op jit(solution)/shard_map/ppermute | solution.py:115
  47.1 0.6 %copy-start.2 = (f32[16,128]{1,0:T(8,128)}, f32[16,128]{1,0:T(8,128)S(1)}, u32[]{:S(2)}) copy-start(f32[16,128]{1,0:T(8,128)S(1)} %collective-permute-done.1.ret_ref) | copy-start | bytes 24580

commit v2 on v0

v2 whole, which is shorter than its diff:
```python
import jax
import jax.numpy as jnp
from jax import lax
from jax.experimental import pallas as pl
from jax.experimental.pallas import tpu as pltpu
from jax.sharding import PartitionSpec as P

SWEEPS, BAND, HALF, LANES = 16, 64, 16, 128
TILE = (16, 128)


def lane_ids(shape=TILE):
    return lax.broadcasted_iota(jnp.int32, shape, len(shape) - 1)


def swap_slots(tiles):
    slot = lane_ids() // HALF
    tiles = list(tiles)
    for s in (4, 2, 1):
        low = slot % (2 * s) < s
        for p in range(8):
            if p & s:
                continue
            a, b = tiles[p], tiles[p | s]
            tiles[p] = jnp.where(low, a, pltpu.roll(b, HALF * s, 1))
            tiles[p | s] = jnp.where(low, pltpu.roll(a, LANES - HALF * s, 1), b)
    return tiles


def pack_kernel(reflectors_ref, copies_ref, turned_ref):
    vectors = reflectors_ref[0]
    first = lax.broadcasted_iota(jnp.int32, vectors.shape, 1) == 0
    vectors = jnp.where(first, jnp.ones_like(vectors), vectors)
    vectors = vectors * jnp.sqrt(2.0 / jnp.sum(vectors * vectors, axis=1, keepdims=True))
    padded = jnp.concatenate([vectors, jnp.zeros_like(vectors)], axis=1)
    padded = jnp.concatenate([padded] + [jnp.zeros_like(padded)] * 3, axis=0)
    turned_ref[...] = padded.T
    slot = lane_ids((8, LANES)) // HALF
    for half in range(2):
        packed = jnp.zeros((8, LANES), jnp.float32)
        for b in range(8):
            entries = turned_ref[pl.ds(b, 8, stride=8), :]
            entries = pltpu.roll(entries, (HALF * (b - half)) % LANES, 1)
            packed = jnp.where(slot == b, entries, packed)
        for sweep in range(SWEEPS):
            copies_ref[sweep, 8 * half : 8 * (half + 1), :] = packed


def pack(reflectors):
    return pl.pallas_call(
        pack_kernel,
        out_shape=jax.ShapeDtypeStruct((SWEEPS, 16, LANES), jnp.float32),
        scratch_shapes=[pltpu.VMEM((LANES, LANES), jnp.float32)],
        name="pack",
    )(reflectors)


def turn_kernel(rows_ref, tiles_ref, gathered_ref):
    for half in range(2):
        for o in range(8):
            for b in range(8):
                gathered_ref[half, o, HALF * b : HALF * (b + 1), :] = rows_ref[
                    pl.ds(half * HALF * BAND + 8 * o + b, HALF, stride=BAND), :
                ]
            turned = gathered_ref[half, o].T
            tiles = swap_slots([turned[HALF * g : HALF * (g + 1)] for g in range(8)])
            for b in range(8):
                tiles_ref[half, 8 * o + b] = tiles[b]


def turn(rows):
    return pl.pallas_call(
        turn_kernel,
        out_shape=jax.ShapeDtypeStruct((2, BAND) + TILE, jnp.float32),
        scratch_shapes=[pltpu.VMEM((2, 8, LANES, LANES), jnp.float32)],
        name="turn",
    )(rows)


def turn_back(state_ref, gathered_ref, out_ref):
    for o in range(8):
        tiles = swap_slots([state_ref[8 * o + b] for b in range(8)])
        gathered_ref[o] = jnp.concatenate(tiles, axis=0).T
        for b in range(8):
            out_ref[pl.ds(8 * o + b, HALF, stride=BAND), :] = gathered_ref[o, HALF * b : HALF * (b + 1), :]


def spread(vectors_ref, half, spread_ref):
    slot = lane_ids((8, LANES)) // HALF
    for sweep in range(SWEEPS):
        packed = vectors_ref[sweep, 8 * half : 8 * (half + 1), :]
        turns = [packed] + [pltpu.roll(packed, HALF * s, 1) for s in range(1, 8)]
        for b in range(8):
            tile = turns[(-b) % 8]
            for g in range(1, 8):
                tile = jnp.where(slot == g, turns[(g - b) % 8], tile)
            spread_ref[sweep, 8 * b : 8 * (b + 1), :] = tile


def entry(spread_ref, sweep, i):
    at = 8 * (i % 8) + i // 8
    return jnp.broadcast_to(spread_ref[sweep, at : at + 1, :], TILE)


def add_up(terms):
    while len(terms) > 1:
        terms = [sum(terms[t + 1 : t + 2], terms[t]) for t in range(0, len(terms), 2)]
    return terms[0]


def sweep_all(state_ref, spread_ref, entering):
    head = lane_ids() % HALF == 0
    sums = [None] * 4

    def add(sums, i, term):
        sums[i % 4] = term if sums[i % 4] is None else sums[i % 4] + term

    for i in range(BAND):
        add(sums, i, entry(spread_ref, SWEEPS - 1, i) * state_ref[SWEEPS - 1 + i])
    total = add_up(sums)
    for sweep in range(SWEEPS - 1, 0, -1):
        last = state_ref[sweep + BAND - 1] - entry(spread_ref, sweep, BAND - 1) * total
        state_ref[sweep + BAND - 1] = last
        first = pltpu.roll(last, 1, 1)
        if entering is not None:
            first = jnp.where(head, entering[sweep - 1], first)
        state_ref[sweep - 1] = first
        sums = [None] * 4
        for i in range(BAND - 1):
            row = state_ref[sweep + i] - entry(spread_ref, sweep, i) * total
            state_ref[sweep + i] = row
            add(sums, i, entry(spread_ref, sweep - 1, i + 1) * row)
        total = add_up(sums) + entry(spread_ref, sweep - 1, 0) * first
    for i in range(BAND):
        state_ref[i] = state_ref[i] - entry(spread_ref, 0, i) * total


def start(tiles_ref, half, after, state_ref):
    tail = lane_ids() % HALF == HALF - 1
    state_ref[:BAND] = tiles_ref[half]
    for i in range(SWEEPS - 1):
        state_ref[BAND + i] = jnp.where(tail, after[i], pltpu.roll(tiles_ref[half, i], LANES - 1, 1))


def halo_tiles(halo_ref, gathered_ref):
    gathered_ref[0, :HALF, :] = halo_ref[...]
    turned = gathered_ref[0].T
    slot = lane_ids() // HALF
    tile = turned[:HALF]
    for g in range(1, 8):
        tile = jnp.where(slot == g, pltpu.roll(turned[HALF * g : HALF * (g + 1)], HALF * g, 1), tile)
    return [pltpu.roll(tile, HALF - 1 - i, 1) for i in range(SWEEPS - 1)]


def leave_kernel(tiles_ref, vectors_ref, halo_ref, leaving_ref, state_ref, spread_ref, gathered_ref):
    gathered_ref[0] = jnp.zeros((LANES, LANES), jnp.float32)
    start(tiles_ref, 1, halo_tiles(halo_ref, gathered_ref), state_ref)
    spread(vectors_ref, 1, spread_ref)
    sweep_all(state_ref, spread_ref, None)
    place = lane_ids() % HALF
    leaving = jnp.zeros(TILE, jnp.float32)
    for i in range(SWEEPS - 1):
        leaving = jnp.where(place == i, pltpu.roll(state_ref[BAND + i], (i - HALF + 1) % LANES, 1), leaving)
    leaving_ref[...] = leaving


STATE = [
    pltpu.VMEM((BAND + SWEEPS,) + TILE, jnp.float32),
    pltpu.VMEM((SWEEPS, BAND, LANES), jnp.float32),
    pltpu.VMEM((8, LANES, LANES), jnp.float32),
]


def leave(tiles, vectors, halo):
    return pl.pallas_call(
        leave_kernel,
        out_shape=jax.ShapeDtypeStruct(TILE, jnp.float32),
        scratch_shapes=STATE,
        name="leave",
    )(tiles, vectors, halo)


def upper_kernel(tiles_ref, vectors_ref, halo_ref, out_ref, lower_ref, state_ref, spread_ref, gathered_ref):
    start(tiles_ref, 0, [pltpu.roll(tiles_ref[1, i], HALF - 1, 1) for i in range(SWEEPS - 1)], lower_ref)
    spread(vectors_ref, 0, spread_ref)
    sweep_all(lower_ref, spread_ref, None)
    gathered_ref[0] = jnp.zeros((LANES, LANES), jnp.float32)
    start(tiles_ref, 1, halo_tiles(halo_ref, gathered_ref), state_ref)
    spread(vectors_ref, 1, spread_ref)
    sweep_all(
        state_ref,
        spread_ref,
        [pltpu.roll(lower_ref[BAND + i], LANES - HALF + 1, 1) for i in range(SWEEPS - 1)],
    )
    turn_back(state_ref, gathered_ref, out_ref)


def upper(tiles, vectors, halo):
    return pl.pallas_call(
        upper_kernel,
        out_shape=jax.ShapeDtypeStruct((2 * HALF * BAND, LANES), jnp.float32),
        grid=(1,),
        in_specs=[pl.BlockSpec(tiles.shape, lambda i: (0, 0, 0, 0)), pl.BlockSpec(vectors.shape, lambda i: (0, 0, 0)), pl.BlockSpec(halo.shape, lambda i: (0, 0))],
        out_specs=pl.BlockSpec((HALF * BAND, LANES), lambda i: (1, 0)),
        scratch_shapes=[STATE[0]] + STATE,
        name="upper",
    )(tiles, vectors, halo)


def lower_kernel(tiles_ref, vectors_ref, entering_ref, upper_ref, out_ref, state_ref, spread_ref, gathered_ref):
    start(tiles_ref, 0, [pltpu.roll(tiles_ref[1, i], HALF - 1, 1) for i in range(SWEEPS - 1)], state_ref)
    spread(vectors_ref, 0, spread_ref)
    entering = entering_ref[...]
    sweep_all(state_ref, spread_ref, [pltpu.roll(entering, (-i) % LANES, 1) for i in range(SWEEPS - 1)])
    turn_back(state_ref, gathered_ref, out_ref)


def lower(tiles, vectors, entering, upper_rows):
    return pl.pallas_call(
        lower_kernel,
        out_shape=jax.ShapeDtypeStruct((2 * HALF * BAND, LANES), jnp.float32),
        grid=(1,),
        in_specs=[pl.BlockSpec(tiles.shape, lambda i: (0, 0, 0, 0)), pl.BlockSpec(vectors.shape, lambda i: (0, 0, 0)), pl.BlockSpec(entering.shape, lambda i: (0, 0)), pl.BlockSpec(memory_space=pl.ANY)],
        out_specs=pl.BlockSpec((HALF * BAND, LANES), lambda i: (0, 0)),
        scratch_shapes=STATE,
        input_output_aliases={3: 0},
        name="lower",
    )(tiles, vectors, entering, upper_rows)


def neighbour(value, step):
    owners = lax.axis_size("row")
    return lax.ppermute(value, "row", [(i, (i + step) % owners) for i in range(owners)])


def local(eigvecs, reflectors):
    copies = pack(reflectors)
    halo = neighbour(eigvecs[:SWEEPS], -1)
    vectors = lax.all_to_all(copies, "col", 0, 0, tiled=True)
    tiles = turn(eigvecs)
    leaving = leave(tiles, vectors, halo)
    entering = neighbour(leaving, 1)
    upper_rows = upper(tiles, vectors, halo)
    return lower(tiles, vectors, entering, upper_rows)


def solution(mesh):
    return jax.shard_map(
        local,
        mesh=mesh,
        in_specs=(P("row", "col"), P("col", "row", None)),
        out_specs=P("row", "col"),
        check_vma=False,
    )
```

time: 993 us -> 45.4 us (0.05)
  the two profiles are of different devices: /device:TPU:6 before, /device:TPU:1 now
where the time goes in v2:
time: 45.4 us; the launch traced here: 45 us
  Pallas kernels  21.4 us (47%)
  starting transfers between devices  21 us (46%)
  local copies, waits for them, and re-layouts  2.53 us (6%)
    all_to_all x1, starting transfers between devices, local(): vectors = lax.all_to_all(copies, 'col', 0, 0, tiled=True)  11.8 us
    ppermute x2, starting transfers between devices, neighbour(): lax.ppermute(value, 'row', [(i, (i + step) % owners) for i in range(owner...  9.21 us
    pallas_call x1, Pallas kernels, upper(): pl.pallas_call(upper_kernel, out_shape=jax.ShapeDtypeStruct((2 * HALF * B...  6.29 us
    pallas_call x1, Pallas kernels, turn(): pl.pallas_call(turn_kernel, out_shape=jax.ShapeDtypeStruct((2, BAND) + TI...  5.35 us
    pallas_call x1, Pallas kernels, lower(): pl.pallas_call(lower_kernel, out_shape=jax.ShapeDtypeStruct((2 * HALF * B...  4.58 us
    pallas_call x1, Pallas kernels, leave(): pl.pallas_call(leave_kernel, out_shape=jax.ShapeDtypeStruct(TILE, jnp.flo...  3.53 us
    unnamed x6, local copies, waits for them, and re-layouts  1.83 us
    pallas_call x1, Pallas kernels, pack(): pl.pallas_call(pack_kernel, out_shape=jax.ShapeDtypeStruct((SWEEPS, 16, L...  1.66 us
  transfers between devices with their start and end apart: 3, of which 0 were waited for; matrix products, arithmetic and copies ran while one was open for 2% of the time, Pallas kernels for 26%

profile of v2, /device:TPU:1, one launch (start us, length us, event | category | flops | bytes accessed | tf_op | source)
XLA Modules:
  0.0 45.0 jit_solution(4861716837891327457)
XLA Ops:
  0.0 1.7 %pack.1 = f32[16,16,128]{2,1,0:T(8,128)} custom-call(f32[1,32,64]{2,1,0:T(8,128)} %reflectors_ref.1), custom_call_target="tpu_custom_call" | custom-call | tf_op jit(solution)/shard_map/pack/pallas_call | solution.py:50
  1.7 11.8 %all-to-all-start = ((f32[16,16,128]{2,1,0:T(8,128)}), f32[16,16,128]{2,1,0:T(8,128)S(1)}, u32[]{:S(2)}, u32[]{:S(2)}) async-start(f32[16,16,128]{2,1,0:T(8,128)} %pack.1), calls=%async_computation | async-start | bytes 262144 | tf_op jit(solution)/shard_map/all_to_all | solution.py:239
  13.5 0.7 %slice.3 = f32[16,128]{1,0:T(8,128)S(1)} slice(f32[2048,128]{1,0:T(8,128)} %rows_ref.1), slice={[0:16], [0:128]} | slice | bytes 16384 | tf_op jit(solution)/shard_map/slice | solution.py:238
  14.2 7.3 %collective-permute-start = (f32[16,128]{1,0:T(8,128)S(1)}, f32[16,128]{1,0:T(8,128)S(1)}, u32[]{:S(2)}, u32[]{:S(2)}) collective-permute-start(f32[16,128]{1,0:T(8,128)S(1)} %slice.3), channel_id=1, source_target_pairs={{0,496},{16,0},{32,16},{48,32},{64,48},{80,64},{96,80},{112,96},{1... | collective-permute-start | bytes 24584 | tf_op jit(solution)/shard_map/ppermute | solution.py:233
  21.5 5.4 %turn.1.tiles_ref = f32[2,64,16,128]{3,2,1,0:T(8,128)} custom-call(f32[2048,128]{1,0:T(8,128)} %rows_ref.1), custom_call_target="tpu_custom_call" | custom-call | tf_op jit(solution)/shard_map/turn/pallas_call | solution.py:72
  26.9 0.0 collective-permute-done.halo_ref
  26.9 0.0 copy-start.1
  26.9 0.0 all-to-all-done.vectors_ref
  26.9 0.6 %copy-done.1 = f32[16,128]{1,0:T(8,128)} copy-done((f32[16,128]{1,0:T(8,128)}, f32[16,128]{1,0:T(8,128)S(1)}, u32[]{:S(2)}) %copy-start.1) | copy-done | bytes 8216
  27.4 0.0 copy-start
  27.4 0.7 %copy-done = f32[16,16,128]{2,1,0:T(8,128)} copy-done((f32[16,16,128]{2,1,0:T(8,128)}, f32[16,16,128]{2,1,0:T(8,128)S(1)}, u32[]{:S(2)}) %copy-start) | copy-done | bytes 131096
  28.1 3.5 %leave.1 = f32[16,128]{1,0:T(8,128)} custom-call(f32[2,64,16,128]{3,2,1,0:T(8,128)} %turn.1.tiles_ref, f32[16,16,128]{2,1,0:T(8,128)} %copy-done, f32[16,128]{1,0:T(8,128)} %copy-done.1), custom_call_target="tpu_custom_call" | custom-call | tf_op jit(solution)/shard_map/leave/pallas_call | solution.py:175
  31.6 1.9 %collective-permute-start.1 = (f32[16,128]{1,0:T(8,128)}, f32[16,128]{1,0:T(8,128)S(1)}, u32[]{:S(2)}, u32[]{:S(2)}) collective-permute-start(f32[16,128]{1,0:T(8,128)} %leave.1), channel_id=1, source_target_pairs={{0,16},{16,32},{32,48},{48,64},{64,80},{80,96},{96,112},{112,128},... | collective-permute-start | bytes 24584 | tf_op jit(solution)/shard_map/ppermute | solution.py:233
  33.5 6.3 %upper.1.upper_ref = f32[2048,128]{1,0:T(8,128)} custom-call(f32[2,64,16,128]{3,2,1,0:T(8,128)} %turn.1.tiles_ref, f32[16,16,128]{2,1,0:T(8,128)} %copy-done, f32[16,128]{1,0:T(8,128)} %copy-done.1), custom_call_target="tpu_custom_call" | custom-call | tf_op jit(solution)/shard_map/upper/pallas_call | solution.py:199
  39.8 0.0 collective-permute-done.1.entering_ref
  39.8 0.0 copy-start.2
  39.8 0.6 %copy-done.2 = f32[16,128]{1,0:T(8,128)} copy-done((f32[16,128]{1,0:T(8,128)}, f32[16,128]{1,0:T(8,128)S(1)}, u32[]{:S(2)}) %copy-start.2) | copy-done | bytes 8216
  40.4 4.6 %lower.1 = f32[2048,128]{1,0:T(8,128)} custom-call(f32[2,64,16,128]{3,2,1,0:T(8,128)} %turn.1.tiles_ref, f32[16,16,128]{2,1,0:T(8,128)} %copy-done, f32[16,128]{1,0:T(8,128)} %copy-done.2, f32[2048,128]{1,0:T(8,128)} %upper.1.upper_ref), custom_call_target="tpu_custom_call", output_to_operand_aliasing={{}: (3, {})} | custom-call | tf_op jit(solution)/shard_map/lower/pallas_call | solution.py:219
Async XLA Ops:
  1.7 25.2 %all-to-all-start = ((f32[16,16,128]{2,1,0:T(8,128)}), f32[16,16,128]{2,1,0:T(8,128)S(1)}, u32[]{:S(2)}, u32[]{:S(2)}) async-start(f32[16,16,128]{2,1,0:T(8,128)} %pack.1), calls=%async_computation | async-start | bytes 262144 | tf_op jit(solution)/shard_map/all_to_all | solution.py:239
  14.2 12.7 %collective-permute-start = (f32[16,128]{1,0:T(8,128)S(1)}, f32[16,128]{1,0:T(8,128)S(1)}, u32[]{:S(2)}, u32[]{:S(2)}) collective-permute-start(f32[16,128]{1,0:T(8,128)S(1)} %slice.3), channel_id=1, source_target_pairs={{0,496},{16,0},{32,16},{48,32},{64,48},{80,64},{96,80},{112,96},{1... | collective-permute-start | bytes 24584 | tf_op jit(solution)/shard_map/ppermute | solution.py:233
  26.9 0.6 %copy-start.1 = (f32[16,128]{1,0:T(8,128)}, f32[16,128]{1,0:T(8,128)S(1)}, u32[]{:S(2)}) copy-start(f32[16,128]{1,0:T(8,128)S(1)} %collective-permute-done.halo_ref) | copy-start | bytes 24580
  27.4 0.7 %copy-start = (f32[16,16,128]{2,1,0:T(8,128)}, f32[16,16,128]{2,1,0:T(8,128)S(1)}, u32[]{:S(2)}) copy-start(f32[16,16,128]{2,1,0:T(8,128)S(1)} %all-to-all-done.vectors_ref) | copy-start | bytes 393220
  31.6 8.2 %collective-permute-start.1 = (f32[16,128]{1,0:T(8,128)}, f32[16,128]{1,0:T(8,128)S(1)}, u32[]{:S(2)}, u32[]{:S(2)}) collective-permute-start(f32[16,128]{1,0:T(8,128)} %leave.1), channel_id=1, source_target_pairs={{0,16},{16,32},{32,48},{48,64},{64,80},{80,96},{96,112},{112,128},... | collective-permute-start | bytes 24584 | tf_op jit(solution)/shard_map/ppermute | solution.py:233
  39.8 0.6 %copy-start.2 = (f32[16,128]{1,0:T(8,128)}, f32[16,128]{1,0:T(8,128)S(1)}, u32[]{:S(2)}) copy-start(f32[16,128]{1,0:T(8,128)S(1)} %collective-permute-done.1.entering_ref) | copy-start | bytes 24580

commit v3 on v2

--- a/solution.py
+++ b/solution.py
@@ -52,6 +52,7 @@
         out_shape=jax.ShapeDtypeStruct((SWEEPS, 16, LANES), jnp.float32),
         scratch_shapes=[pltpu.VMEM((LANES, LANES), jnp.float32)],
         name="pack",
+        compiler_params=pltpu.CompilerParams(vmem_limit_bytes=8 * 2**20),
     )(reflectors)
 
 
@@ -74,6 +75,7 @@
         out_shape=jax.ShapeDtypeStruct((2, BAND) + TILE, jnp.float32),
         scratch_shapes=[pltpu.VMEM((2, 8, LANES, LANES), jnp.float32)],
         name="turn",
+        compiler_params=pltpu.CompilerParams(vmem_limit_bytes=8 * 2**20),
     )(rows)
 
 
@@ -177,6 +179,7 @@
         out_shape=jax.ShapeDtypeStruct(TILE, jnp.float32),
         scratch_shapes=STATE,
         name="leave",
+        compiler_params=pltpu.CompilerParams(vmem_limit_bytes=8 * 2**20),
     )(tiles, vectors, halo)
 
 
@@ -204,6 +207,7 @@
         out_specs=pl.BlockSpec((HALF * BAND, LANES), lambda i: (1, 0)),
         scratch_shapes=[STATE[0]] + STATE,
         name="upper",
+        compiler_params=pltpu.CompilerParams(vmem_limit_bytes=8 * 2**20),
     )(tiles, vectors, halo)
 
 
@@ -225,6 +229,7 @@
         scratch_shapes=STATE,
         input_output_aliases={3: 0},
         name="lower",
+        compiler_params=pltpu.CompilerParams(vmem_limit_bytes=8 * 2**20),
     )(tiles, vectors, entering, upper_rows)
 
 

time: 45.4 us -> 38.9 us (0.86)
  Pallas kernels: 21.4 us -> 14 us
  waiting for transfers between devices: 0.01 us -> 0.81 us
    pallas_call x1, Pallas kernels: 5.35 us -> 3.17 us  [turn(): pl.pallas_call(turn_kernel, out_shape=jax.ShapeDtypeStruct((2, BAND) + TI...]
    pallas_call x1, Pallas kernels: 3.53 us -> 1.62 us  [leave(): pl.pallas_call(leave_kernel, out_shape=jax.ShapeDtypeStruct(TILE, jnp.flo...]
    pallas_call x1, Pallas kernels: 4.58 us -> 3.27 us  [lower(): pl.pallas_call(lower_kernel, out_shape=jax.ShapeDtypeStruct((2 * HALF * B...]
    pallas_call x1, Pallas kernels: 6.29 us -> 4.98 us  [upper(): pl.pallas_call(upper_kernel, out_shape=jax.ShapeDtypeStruct((2 * HALF * B...]
    ppermute x2, waiting for transfers between devices: 0.01 us -> 0.81 us  [neighbour(): lax.ppermute(value, 'row', [(i, (i + step) % owners) for i in range(owner...]
    pallas_call x1, Pallas kernels: 1.66 us -> 0.94 us  [pack(): pl.pallas_call(pack_kernel, out_shape=jax.ShapeDtypeStruct((SWEEPS, 16, L...]
    unnamed x6 -> x4, local copies, waits for them, and re-layouts: 1.83 us -> 1.94 us
  transfers between devices with their start and end apart: 3 -> 3, of which waited for: 0 -> 1; matrix products, arithmetic and copies ran while one was open for 2% -> 2% of each run, Pallas kernels for 26% -> 21%
where the time goes in v3:
time: 38.9 us; the launch traced here: 38.5 us
  starting transfers between devices  21.1 us (54%)
  Pallas kernels  14 us (36%)
  local copies, waits for them, and re-layouts  2.63 us (7%)
  waiting for transfers between devices  0.81 us (2%)
    all_to_all x1, starting transfers between devices, local(): vectors = lax.all_to_all(copies, 'col', 0, 0, tiled=True)  11.8 us
    ppermute x2, starting transfers between devices, neighbour(): lax.ppermute(value, 'row', [(i, (i + step) % owners) for i in range(owner...  9.22 us
    pallas_call x1, Pallas kernels, upper(): pl.pallas_call(upper_kernel, out_shape=jax.ShapeDtypeStruct((2 * HALF * B...  4.98 us
    pallas_call x1, Pallas kernels, lower(): pl.pallas_call(lower_kernel, out_shape=jax.ShapeDtypeStruct((2 * HALF * B...  3.27 us
    pallas_call x1, Pallas kernels, turn(): pl.pallas_call(turn_kernel, out_shape=jax.ShapeDtypeStruct((2, BAND) + TI...  3.17 us
    unnamed x4, local copies, waits for them, and re-layouts  1.94 us
    pallas_call x1, Pallas kernels, leave(): pl.pallas_call(leave_kernel, out_shape=jax.ShapeDtypeStruct(TILE, jnp.flo...  1.62 us
    pallas_call x1, Pallas kernels, pack(): pl.pallas_call(pack_kernel, out_shape=jax.ShapeDtypeStruct((SWEEPS, 16, L...  0.94 us
  transfers between devices with their start and end apart: 3, of which 1 were waited for; matrix products, arithmetic and copies ran while one was open for 2% of the time, Pallas kernels for 21%

profile of v3, /device:TPU:1, one launch (start us, length us, event | category | flops | bytes accessed | tf_op | source)
XLA Modules:
  0.0 38.5 jit_solution(7768756349592050536)
XLA Ops:
  0.0 0.0 copy-start.1
  0.0 0.7 %copy-done.1 = f32[1,32,64]{2,1,0:T(8,128)S(1)} copy-done((f32[1,32,64]{2,1,0:T(8,128)S(1)}, f32[1,32,64]{2,1,0:T(8,128)}, u32[]{:S(2)}) %copy-start.1) | copy-done | bytes 8216
  0.7 0.9 %pack.1 = f32[16,16,128]{2,1,0:T(8,128)} custom-call(f32[1,32,64]{2,1,0:T(8,128)S(1)} %copy-done.1), custom_call_target="tpu_custom_call" | custom-call | tf_op jit(solution)/shard_map/pack/pallas_call | solution.py:50
  1.7 11.8 %all-to-all-start = ((f32[16,16,128]{2,1,0:T(8,128)}), f32[16,16,128]{2,1,0:T(8,128)S(1)}, u32[]{:S(2)}, u32[]{:S(2)}) async-start(f32[16,16,128]{2,1,0:T(8,128)} %pack.1), calls=%async_computation | async-start | bytes 262144 | tf_op jit(solution)/shard_map/all_to_all | solution.py:244
  13.5 0.7 %slice.3 = f32[16,128]{1,0:T(8,128)S(1)} slice(f32[2048,128]{1,0:T(8,128)} %rows_ref.1), slice={[0:16], [0:128]} | slice | bytes 16384 | tf_op jit(solution)/shard_map/slice | solution.py:243
  14.2 7.3 %collective-permute-start = (f32[16,128]{1,0:T(8,128)S(1)}, f32[16,128]{1,0:T(8,128)S(1)}, u32[]{:S(2)}, u32[]{:S(2)}) collective-permute-start(f32[16,128]{1,0:T(8,128)S(1)} %slice.3), channel_id=1, source_target_pairs={{0,496},{16,0},{32,16},{48,32},{64,48},{80,64},{96,80},{112,96},{1... | collective-permute-start | bytes 24584 | tf_op jit(solution)/shard_map/ppermute | solution.py:238
  21.5 0.0 copy-start
  21.5 1.2 %copy-done = f32[2048,128]{1,0:T(8,128)S(1)} copy-done((f32[2048,128]{1,0:T(8,128)S(1)}, f32[2048,128]{1,0:T(8,128)}, u32[]{:S(2)}) %copy-start) | copy-done | bytes 1048600
  22.7 3.2 %turn.1.tiles_ref = f32[2,64,16,128]{3,2,1,0:T(8,128)S(1)} custom-call(f32[2048,128]{1,0:T(8,128)S(1)} %copy-done), custom_call_target="tpu_custom_call" | custom-call | tf_op jit(solution)/shard_map/turn/pallas_call | solution.py:73
  25.9 0.0 collective-permute-done.halo_ref
  25.9 0.0 all-to-all-done.vectors_ref
  25.9 1.6 %leave.1 = f32[16,128]{1,0:T(8,128)S(1)} custom-call(f32[2,64,16,128]{3,2,1,0:T(8,128)S(1)} %turn.1.tiles_ref, f32[16,16,128]{2,1,0:T(8,128)S(1)} %all-to-all-done.vectors_ref, f32[16,128]{1,0:T(8,128)S(1)} %collective-permute-done.halo_ref), custom_call_target="tpu_custom_call" | custom-call | tf_op jit(solution)/shard_map/leave/pallas_call | solution.py:177
  27.6 1.9 %collective-permute-start.1 = (f32[16,128]{1,0:T(8,128)S(1)}, f32[16,128]{1,0:T(8,128)S(1)}, u32[]{:S(2)}, u32[]{:S(2)}) collective-permute-start(f32[16,128]{1,0:T(8,128)S(1)} %leave.1), channel_id=1, source_target_pairs={{0,16},{16,32},{32,48},{48,64},{64,80},{80,96},{96,112},{112,128},... | collective-permute-start | bytes 24584 | tf_op jit(solution)/shard_map/ppermute | solution.py:238
  29.5 5.0 %upper.1.upper_ref = f32[2048,128]{1,0:T(8,128)} custom-call(f32[2,64,16,128]{3,2,1,0:T(8,128)S(1)} %turn.1.tiles_ref, f32[16,16,128]{2,1,0:T(8,128)S(1)} %all-to-all-done.vectors_ref, f32[16,128]{1,0:T(8,128)S(1)} %collective-permute-done.halo_ref), custom_call_target="tpu_custom_call" | custom-call | tf_op jit(solution)/shard_map/upper/pallas_call | solution.py:202
  34.5 0.8 %collective-permute-done.1.entering_ref = f32[16,128]{1,0:T(8,128)S(1)} collective-permute-done((f32[16,128]{1,0:T(8,128)S(1)}, f32[16,128]{1,0:T(8,128)S(1)}, u32[]{:S(2)}, u32[]{:S(2)}) %collective-permute-start.1) | collective-permute-done | bytes 8224 | tf_op jit(solution)/shard_map/ppermute | solution.py:238
  35.3 3.3 %lower.1 = f32[2048,128]{1,0:T(8,128)} custom-call(f32[2,64,16,128]{3,2,1,0:T(8,128)S(1)} %turn.1.tiles_ref, f32[16,16,128]{2,1,0:T(8,128)S(1)} %all-to-all-done.vectors_ref, f32[16,128]{1,0:T(8,128)S(1)} %collective-permute-done.1.entering_ref, f32[2048,128]{1,0:T(8,128)} %upper.1.upper_ref), custom_call_target="tpu_custom_call", output_to_operand_aliasing={{}: (3, {})} | custom-call | tf_op jit(solution)/shard_map/lower/pallas_call | solution.py:223
Async XLA Ops:
  0.0 0.7 %copy-start.1 = (f32[1,32,64]{2,1,0:T(8,128)S(1)}, f32[1,32,64]{2,1,0:T(8,128)}, u32[]{:S(2)}) copy-start(f32[1,32,64]{2,1,0:T(8,128)} %reflectors_ref.1) | copy-start | bytes 24580
  1.7 24.3 %all-to-all-start = ((f32[16,16,128]{2,1,0:T(8,128)}), f32[16,16,128]{2,1,0:T(8,128)S(1)}, u32[]{:S(2)}, u32[]{:S(2)}) async-start(f32[16,16,128]{2,1,0:T(8,128)} %pack.1), calls=%async_computation | async-start | bytes 262144 | tf_op jit(solution)/shard_map/all_to_all | solution.py:244
  14.2 11.7 %collective-permute-start = (f32[16,128]{1,0:T(8,128)S(1)}, f32[16,128]{1,0:T(8,128)S(1)}, u32[]{:S(2)}, u32[]{:S(2)}) collective-permute-start(f32[16,128]{1,0:T(8,128)S(1)} %slice.3), channel_id=1, source_target_pairs={{0,496},{16,0},{32,16},{48,32},{64,48},{80,64},{96,80},{112,96},{1... | collective-permute-start | bytes 24584 | tf_op jit(solution)/shard_map/ppermute | solution.py:238
  21.5 1.2 %copy-start = (f32[2048,128]{1,0:T(8,128)S(1)}, f32[2048,128]{1,0:T(8,128)}, u32[]{:S(2)}) copy-start(f32[2048,128]{1,0:T(8,128)} %rows_ref.1) | copy-start | bytes 3145732
  27.6 7.7 %collective-permute-start.1 = (f32[16,128]{1,0:T(8,128)S(1)}, f32[16,128]{1,0:T(8,128)S(1)}, u32[]{:S(2)}, u32[]{:S(2)}) collective-permute-start(f32[16,128]{1,0:T(8,128)S(1)} %leave.1), channel_id=1, source_target_pairs={{0,16},{16,32},{32,48},{48,64},{64,80},{80,96},{96,112},{112,128},... | collective-permute-start | bytes 24584 | tf_op jit(solution)/shard_map/ppermute | solution.py:238

commit v4 on v2

v4 whole, which is shorter than its diff:
```python
import jax
import jax.numpy as jnp
from jax import lax
from jax.experimental import pallas as pl
from jax.experimental.pallas import tpu as pltpu
from jax.sharding import PartitionSpec as P

SWEEPS, BAND, HALF, LANES = 16, 64, 16, 128
TILE = (16, 128)
EARLY = 6


def is_early():
    row, column = lax.axis_index("row"), lax.axis_index("col")
    return jnp.logical_and(column < EARLY, row + column > 0)


PARAMS = pltpu.CompilerParams(vmem_limit_bytes=8 * 2**20)


def lane_ids(shape=TILE):
    return lax.broadcasted_iota(jnp.int32, shape, len(shape) - 1)


def swap_slots(tiles):
    slot = lane_ids() // HALF
    skewed = [pltpu.roll(tiles[p], HALF * p, 1) if p else tiles[p] for p in range(8)]
    skewed = [skewed[-t % 8] for t in range(8)]
    for s in (1, 2, 4):
        moved = slot & s != 0
        skewed = [jnp.where(moved, skewed[(t - s) % 8], skewed[t]) for t in range(8)]
    return [pltpu.roll(skewed[q], LANES - HALF * q, 1) if q else skewed[q] for q in range(8)]


def pack_kernel(reflectors_ref, copies_ref, turned_ref):
    vectors = reflectors_ref[0]
    first = lax.broadcasted_iota(jnp.int32, vectors.shape, 1) == 0
    vectors = jnp.where(first, jnp.ones_like(vectors), vectors)
    vectors = vectors * jnp.sqrt(2.0 / jnp.sum(vectors * vectors, axis=1, keepdims=True))
    padded = jnp.concatenate([vectors, jnp.zeros_like(vectors)], axis=1)
    padded = jnp.concatenate([padded] + [jnp.zeros_like(padded)] * 3, axis=0)
    turned_ref[...] = padded.T
    slot = lane_ids((8, LANES)) // HALF
    for half in range(2):
        packed = jnp.zeros((8, LANES), jnp.float32)
        for b in range(8):
            entries = turned_ref[pl.ds(b, 8, stride=8), :]
            entries = pltpu.roll(entries, (HALF * (b - half)) % LANES, 1)
            packed = jnp.where(slot == b, entries, packed)
        for sweep in range(SWEEPS):
            copies_ref[sweep, 8 * half : 8 * (half + 1), :] = packed


def pack(reflectors):
    return pl.pallas_call(
        pack_kernel,
        out_shape=jax.ShapeDtypeStruct((SWEEPS, 16, LANES), jnp.float32),
        scratch_shapes=[pltpu.VMEM((LANES, LANES), jnp.float32)],
        name="pack",
        compiler_params=PARAMS,
    )(reflectors)


def turn_rows(rows_ref, landed_ref, gathered_ref, tiles_ref, arrived):
    pieces = [pl.ds(half * HALF * BAND, HALF * BAND) for half in range(2)]
    copies = [
        pltpu.make_async_copy(rows_ref.at[piece], landed_ref.at[piece], arrived.at[half])
        for half, piece in enumerate(pieces)
    ]
    for copy in copies:
        copy.start()
    for half in range(2):
        copies[half].wait()
        for o in range(8):
            for b in range(8):
                gathered_ref[half, o, HALF * b : HALF * (b + 1), :] = landed_ref[
                    pl.ds(half * HALF * BAND + 8 * o + b, HALF, stride=BAND), :
                ]
            turned = gathered_ref[half, o].T
            tiles = swap_slots([turned[HALF * g : HALF * (g + 1)] for g in range(8)])
            for b in range(8):
                tiles_ref[half, 8 * o + b] = tiles[b]


def turn_early_kernel(rows_ref, tiles_ref, landed_ref, gathered_ref, arrived, turned_ref, left):
    @pl.when(is_early())
    def _():
        turn_rows(rows_ref, landed_ref, gathered_ref, turned_ref, arrived)
        copy = pltpu.make_async_copy(turned_ref, tiles_ref, left)
        copy.start()
        copy.wait()


def turn_late_kernel(rows_ref, early_ref, tiles_ref, *scratch):
    arrived = scratch[2]
    @pl.when(jnp.logical_not(is_early()))
    def _():
        turn_rows(rows_ref, scratch[0], scratch[1], tiles_ref, scratch[2])

    @pl.when(is_early())
    def _():
        copies = [pltpu.make_async_copy(early_ref.at[half], tiles_ref.at[half], arrived.at[half]) for half in range(2)]
        for copy in copies:
            copy.start()
        for copy in copies:
            copy.wait()


TURN = dict(
    out_shape=jax.ShapeDtypeStruct((2, BAND) + TILE, jnp.float32),
    scratch_shapes=[
        pltpu.VMEM((2 * HALF * BAND, LANES), jnp.float32),
        pltpu.VMEM((2, 8, LANES, LANES), jnp.float32),
        pltpu.SemaphoreType.DMA((2,)),
    ],
    compiler_params=PARAMS,
)


def turn_early(rows):
    return pl.pallas_call(
        turn_early_kernel,
        out_shape=TURN["out_shape"],
        in_specs=[pl.BlockSpec(memory_space=pl.ANY)],
        out_specs=pl.BlockSpec(memory_space=pl.ANY),
        scratch_shapes=TURN["scratch_shapes"] + [pltpu.VMEM((2, BAND) + TILE, jnp.float32), pltpu.SemaphoreType.DMA],
        name="turn_early",
        compiler_params=pltpu.CompilerParams(vmem_limit_bytes=56 * 2**20),
    )(rows)


def turn_late(rows, early):
    return pl.pallas_call(
        turn_late_kernel,
        in_specs=[pl.BlockSpec(memory_space=pl.ANY)] * 2,
        name="turn_late",
        **TURN,
    )(rows, early)


def turn_back(turned, rows_ref, out_ref, half, o, sent):
    rows = turned.T
    for b in range(8):
        rows_ref[o, pl.ds(b, HALF, stride=8), :] = rows[HALF * b : HALF * (b + 1)]
    copy = pltpu.make_async_copy(
        rows_ref.at[o].reshape(HALF, 8, LANES),
        out_ref.at[pl.ds(HALF * half, HALF), pl.ds(8 * o, 8)],
        sent.at[o],
    )
    copy.start()
    return copy


def rows_after(state_ref):
    place = lane_ids() % HALF
    tile = jnp.zeros(TILE, jnp.float32)
    for i in range(SWEEPS - 1):
        tile = jnp.where(place == i, pltpu.roll(state_ref[BAND + i], (i - HALF + 1) % LANES, 1), tile)
    return tile


def spread(vectors_ref, half, sweep):
    slot = lane_ids((8, LANES)) // HALF
    packed = vectors_ref[sweep, 8 * half : 8 * (half + 1), :]
    turns = [packed] + [pltpu.roll(packed, HALF * s, 1) for s in range(1, 8)]
    tiles = []
    for b in range(8):
        tile = turns[(-b) % 8]
        for g in range(1, 8):
            tile = jnp.where(slot == g, turns[(g - b) % 8], tile)
        tiles.append(tile)
    return tiles


def add_up(terms):
    while len(terms) > 1:
        terms = [sum(terms[t + 1 : t + 2], terms[t]) for t in range(0, len(terms), 2)]
    return terms[0]


def sweep_all(state_ref, spread_ref, prepare, entering, beside):
    tile = state_ref.shape[1:]
    head = lane_ids(tile) % HALF == 0
    sums = [None] * 4
    beside = list(beside)
    share = -(-len(beside) // (SWEEPS - 1))

    def entry(sweep, i):
        at = 8 * (i % 8) + i // 8
        return jnp.broadcast_to(spread_ref[sweep, at : at + 1, :], tile)

    def add(sums, i, term):
        sums[i % 4] = term if sums[i % 4] is None else sums[i % 4] + term

    for sweep in range(SWEEPS - 1, -1, -1):
        prepare(sweep)
    for i in range(BAND):
        add(sums, i, entry(SWEEPS - 1, i) * state_ref[SWEEPS - 1 + i])
    total = add_up(sums)
    for sweep in range(SWEEPS - 1, 0, -1):
        last = state_ref[sweep + BAND - 1] - entry(sweep, BAND - 1) * total
        state_ref[sweep + BAND - 1] = last
        first = jnp.where(head, entering(sweep - 1), pltpu.roll(last, 1, 1))
        state_ref[sweep - 1] = first
        sums = [None] * 4
        for i in range(BAND - 1):
            row = state_ref[sweep + i] - entry(sweep, i) * total
            state_ref[sweep + i] = row
            add(sums, i, entry(sweep - 1, i + 1) * row)
        total = add_up(sums) + entry(sweep - 1, 0) * first
        for work in beside[:share]:
            work()
        beside = beside[share:]
    for i in range(BAND):
        state_ref[i] = state_ref[i] - entry(0, i) * total


def nothing(i):
    return jnp.zeros(TILE, jnp.float32)


def after_kernel(tiles_ref, halo_ref, after_ref, gathered_ref):
    last = lane_ids() % HALF == HALF - 1
    gathered_ref[...] = jnp.zeros_like(gathered_ref)
    gathered_ref[:HALF, :] = halo_ref[...]
    turned = gathered_ref[...].T
    slot = lane_ids() // HALF
    halo = turned[:HALF]
    for g in range(1, 8):
        halo = jnp.where(slot == g, pltpu.roll(turned[HALF * g : HALF * (g + 1)], HALF * g, 1), halo)
    for i in range(SWEEPS - 1):
        own = [pltpu.roll(tiles_ref[half, i], LANES - 1, 1) for half in range(2)]
        after_ref[0, i] = jnp.where(last, pltpu.roll(tiles_ref[1, i], HALF - 1, 1), own[0])
        after_ref[1, i] = jnp.where(last, pltpu.roll(halo, HALF - 1 - i, 1), own[1])


def rows_following(tiles, halo):
    return pl.pallas_call(
        after_kernel,
        out_shape=jax.ShapeDtypeStruct((2, SWEEPS - 1) + TILE, jnp.float32),
        scratch_shapes=[pltpu.VMEM((LANES, LANES), jnp.float32)],
        name="after",
        compiler_params=PARAMS,
    )(tiles, halo)


def leave_kernel(tiles_ref, vectors_ref, after_ref, leaving_ref, spread_ref, state_ref):
    state_ref[:BAND] = tiles_ref[1]
    state_ref[BAND : BAND + SWEEPS - 1] = after_ref[1]

    def prepare(sweep):
        for b, tile in enumerate(spread(vectors_ref, 1, sweep)):
            spread_ref[sweep, 8 * b : 8 * (b + 1), :] = tile

    sweep_all(state_ref, spread_ref, prepare, nothing, [])
    leaving_ref[...] = rows_after(state_ref)


STATE, SPREAD = (BAND + SWEEPS,) + TILE, (SWEEPS, BAND, LANES)
OCTS = (8, LANES, LANES)
OUT = (2 * HALF, BAND, LANES)
VMEM, ANY = pl.BlockSpec(memory_space=pltpu.VMEM), pl.BlockSpec(memory_space=pl.ANY)


def leave(tiles, vectors, after):
    return pl.pallas_call(
        leave_kernel,
        out_shape=tuple(jax.ShapeDtypeStruct(shape, jnp.float32) for shape in (TILE, SPREAD)),
        scratch_shapes=[pltpu.VMEM(STATE, jnp.float32)],
        name="leave",
        compiler_params=PARAMS,
    )(tiles, vectors, after)


def upper_kernel(
    tiles_ref, vectors_ref, after_ref, upper_spread_ref,
    out_ref, fixed_ref, response_ref,
    lower_ref, state_ref, spread_ref, rows_ref, sent,
):
    lower_ref[:, 16:, :] = jnp.zeros((BAND + SWEEPS, 8, LANES), jnp.float32)
    for i in range(BAND):
        lower_ref[i, :16, :] = tiles_ref[0, i]
    for i in range(SWEEPS - 1):
        lower_ref[BAND + i, :16, :] = after_ref[0, i]

    def prepare(sweep):
        for b, tile in enumerate(spread(vectors_ref, 0, sweep)):
            spread_ref[sweep, 8 * b : 8 * (b + 1), :] = tile

    wide = lower_ref.shape[1:]
    row, parity = lax.broadcasted_iota(jnp.int32, wide, 0), lane_ids(wide) // HALF % 2
    sweep_all(
        lower_ref,
        spread_ref,
        prepare,
        lambda i: jnp.where(jnp.logical_and(row == 16 + i % 8, parity == i // 8), 1.0, 0.0),
        [],
    )
    state_ref[:BAND] = tiles_ref[1]
    state_ref[BAND : BAND + SWEEPS - 1] = after_ref[1]
    sweep_all(
        state_ref,
        upper_spread_ref,
        lambda sweep: None,
        lambda i: pltpu.roll(lower_ref[BAND + i, :16, :], LANES - HALF + 1, 1),
        [],
    )
    copies = []
    for o in range(8):
        turned = jnp.concatenate(swap_slots([state_ref[8 * o + b] for b in range(8)]), axis=0)
        copies.append(turn_back(turned, rows_ref, out_ref, 1, o, sent))
    slot = lane_ids((8, LANES)) // HALF
    for o in range(8):
        fixed_ref[o] = jnp.concatenate(swap_slots([lower_ref[8 * o + b, :16, :] for b in range(8)]), axis=0)
        first, second = None, None
        for b in range(8):
            unit = lower_ref[8 * o + b, 16:, :]
            parts = unit, pltpu.roll(unit, HALF, 1)
            first = parts[0] if first is None else jnp.where(slot == b, parts[b % 2], first)
            second = parts[1] if second is None else jnp.where(slot == b, parts[1 - b % 2], second)
        response_ref[o, :8, :] = first
        response_ref[o, 8:, :] = second
    for copy in copies:
        copy.wait()


def upper(*operands):
    return pl.pallas_call(
        upper_kernel,
        out_shape=tuple(jax.ShapeDtypeStruct(shape, jnp.float32) for shape in (OUT, OCTS, (8,) + TILE)),
        out_specs=(ANY, VMEM, VMEM),
        scratch_shapes=[pltpu.VMEM(shape, jnp.float32) for shape in ((BAND + SWEEPS, 24, LANES), STATE, SPREAD, OCTS)]
        + [pltpu.SemaphoreType.DMA((8,))],
        name="upper",
        compiler_params=PARAMS,
    )(*operands)


def lower_kernel(fixed_ref, response_ref, entering_ref, upper_ref, out_ref, rows_ref, sent):
    tile = entering_ref[...]
    valid = lane_ids() % HALF < SWEEPS - 1
    tile = jnp.where(valid, tile, jnp.zeros_like(tile))
    entering = jnp.concatenate(
        [tile] + [pltpu.roll(tile, LANES - HALF * g, 1) for g in range(1, 8)], axis=0
    )[:, :HALF]
    copies = []
    for o in range(8):
        added = lax.dot_general(
            entering,
            response_ref[o],
            (((1,), (0,)), ((), ())),
            precision=lax.Precision.HIGHEST,
            preferred_element_type=jnp.float32,
        )
        copies.append(turn_back(fixed_ref[o] + added, rows_ref, out_ref, 0, o, sent))
    for copy in copies:
        copy.wait()


def lower(fixed, response, entering, upper_rows):
    return pl.pallas_call(
        lower_kernel,
        out_shape=jax.ShapeDtypeStruct(OUT, jnp.float32),
        in_specs=[VMEM, VMEM, VMEM, ANY],
        out_specs=ANY,
        scratch_shapes=[pltpu.VMEM(OCTS, jnp.float32), pltpu.SemaphoreType.DMA((8,))],
        input_output_aliases={3: 0},
        name="lower",
        compiler_params=PARAMS,
    )(fixed, response, entering, upper_rows)


def neighbour(value, step):
    owners = lax.axis_size("row")
    return lax.ppermute(value, "row", [(i, (i + step) % owners) for i in range(owners)])


def local(eigvecs, reflectors):
    early, copies = lax.optimization_barrier((turn_early(eigvecs), pack(reflectors)))
    vectors = lax.all_to_all(copies, "col", 0, 0, tiled=True)
    halo = neighbour(eigvecs[:SWEEPS], -1)
    return sweeps(eigvecs, early, halo, vectors)


def sweeps(eigvecs, early, halo, vectors):
    tiles = turn_late(eigvecs, early)
    after = rows_following(tiles, halo)
    leaving, upper_spread = leave(tiles, vectors, after)
    entering = neighbour(leaving, 1)
    upper_rows, fixed, response = upper(tiles, vectors, after, upper_spread)
    return lower(fixed, response, entering, upper_rows).reshape(eigvecs.shape)


def solution(mesh):
    return jax.shard_map(
        local,
        mesh=mesh,
        in_specs=(P("row", "col"), P("col", "row", None)),
        out_specs=P("row", "col"),
        check_vma=False,
    )
```

time: 45.4 us -> 34.8 us (0.77)
  the two profiles are of different devices: /device:TPU:1 before, /device:TPU:27 now
where the time goes in v4:
time: 34.8 us; the launch traced here: 34.4 us
  starting transfers between devices  13.8 us (40%)
  Pallas kernels  13.2 us (38%)
  waiting for transfers between devices  5.39 us (15%)
  local copies, waits for them, and re-layouts  1.94 us (6%)
    all_to_all x1, starting transfers between devices, local(): vectors = lax.all_to_all(copies, 'col', 0, 0, tiled=True)  7.27 us
    ppermute x2, starting transfers between devices, neighbour(): lax.ppermute(value, 'row', [(i, (i + step) % owners) for i in range(owner...  6.52 us
    pallas_call x1, Pallas kernels, upper(): pl.pallas_call(upper_kernel, out_shape=tuple((jax.ShapeDtypeStruct(shape,...  5.05 us
    pallas_call x1, Pallas kernels, turn_early(): pl.pallas_call(turn_early_kernel, out_shape=TURN['out_shape'], in_specs=[...  3.91 us
    all_to_all x1, waiting for transfers between devices, local(): vectors = lax.all_to_all(copies, 'col', 0, 0, tiled=True)  2.9 us
    ppermute x2, waiting for transfers between devices, neighbour(): lax.ppermute(value, 'row', [(i, (i + step) % owners) for i in range(owner...  2.49 us
    unnamed x6, local copies, waits for them, and re-layouts  1.94 us
    pallas_call x1, Pallas kernels, leave(): pl.pallas_call(leave_kernel, out_shape=tuple((jax.ShapeDtypeStruct(shape,...  1.5 us
  transfers between devices with their start and end apart: 3, of which 2 were waited for; matrix products, arithmetic and copies ran while one was open for 0% of the time, Pallas kernels for 16%

profile of v4, /device:TPU:27, one launch (start us, length us, event | category | flops | bytes accessed | tf_op | source)
XLA Modules:
  0.0 34.4 jit_solution(16295143390103694182)
XLA Ops:
  0.0 0.0 copy-start.2
  0.0 0.7 %copy-done.2 = f32[1,32,64]{2,1,0:T(8,128)S(1)} copy-done((f32[1,32,64]{2,1,0:T(8,128)S(1)}, f32[1,32,64]{2,1,0:T(8,128)}, u32[]{:S(2)}) %copy-start.2) | copy-done | bytes 8216
  0.7 0.9 %pack.1 = f32[16,16,128]{2,1,0:T(8,128)} custom-call(f32[1,32,64]{2,1,0:T(8,128)S(1)} %copy-done.2), custom_call_target="tpu_custom_call" | custom-call | tf_op jit(solution)/shard_map/pack/pallas_call | solution.py:55
  1.7 0.0 copy-start
  1.7 3.9 %turn_early.1.early_ref = f32[2,64,16,128]{3,2,1,0:T(8,128)} custom-call(f32[2048,128]{1,0:T(8,128)} %rows_ref.3), custom_call_target="tpu_custom_call" | custom-call | tf_op jit(solution)/shard_map/turn_early/pallas_call | solution.py:121
  5.6 7.3 %all-to-all-start = ((f32[16,16,128]{2,1,0:T(8,128)}), f32[16,16,128]{2,1,0:T(8,128)S(1)}, u32[]{:S(2)}, u32[]{:S(2)}) async-start(f32[16,16,128]{2,1,0:T(8,128)} %pack.1), calls=%async_computation | async-start | bytes 262144 | tf_op jit(solution)/shard_map/all_to_all | solution.py:380
  12.8 0.0 copy-done
  12.9 2.1 %collective-permute-start = (f32[16,128]{1,0:T(8,128)S(1)}, f32[16,128]{1,0:T(8,128)S(1)}, u32[]{:S(2)}, u32[]{:S(2)}) collective-permute-start(f32[16,128]{1,0:T(8,128)S(1)} %slice.3), channel_id=1, source_target_pairs={{0,496},{16,0},{32,16},{48,32},{64,48},{80,64},{96,80},{112,96},{1... | collective-permute-start | bytes 24584 | tf_op jit(solution)/shard_map/ppermute | solution.py:375
  15.0 0.0 copy-start.1
  15.0 1.2 %copy-done.1 = f32[2,64,16,128]{3,2,1,0:T(8,128)S(1)} copy-done((f32[2,64,16,128]{3,2,1,0:T(8,128)S(1)}, f32[2,64,16,128]{3,2,1,0:T(8,128)}, u32[]{:S(2)}) %copy-start.1) | copy-done | bytes 1048600
  16.2 0.1 turn_late.1.tiles_ref
  16.3 2.5 %collective-permute-done.halo_ref = f32[16,128]{1,0:T(8,128)S(1)} collective-permute-done((f32[16,128]{1,0:T(8,128)S(1)}, f32[16,128]{1,0:T(8,128)S(1)}, u32[]{:S(2)}, u32[]{:S(2)}) %collective-permute-start) | collective-permute-done | bytes 8224 | tf_op jit(solution)/shard_map/ppermute | solution.py:375
  18.8 0.3 after.1.after_ref
  19.1 2.9 %all-to-all-done.vectors_ref = f32[16,16,128]{2,1,0:T(8,128)S(1)} async-done(((f32[16,16,128]{2,1,0:T(8,128)}), f32[16,16,128]{2,1,0:T(8,128)S(1)}, u32[]{:S(2)}, u32[]{:S(2)}) %all-to-all-start) | async-done | bytes 131104 | tf_op jit(solution)/shard_map/all_to_all | solution.py:380
  22.0 1.5 %leave.1 = (f32[16,128]{1,0:T(8,128)S(1)}, f32[16,64,128]{2,1,0:T(8,128)S(1)}) custom-call(f32[2,64,16,128]{3,2,1,0:T(8,128)S(1)} %turn_late.1.tiles_ref, f32[16,16,128]{2,1,0:T(8,128)S(1)} %all-to-all-done.vectors_ref, f32[2,15,16,128]{3,2,1,0:T(8,128)S(1)} %after.1.after_ref), custom_call_target="tpu_custom_call" | custom-call | tf_op jit(solution)/shard_map/leave/pallas_call | solution.py:266
  23.5 4.4 %collective-permute-start.1 = (f32[16,128]{1,0:T(8,128)S(1)}, f32[16,128]{1,0:T(8,128)S(1)}, u32[]{:S(2)}, u32[]{:S(2)}) collective-permute-start(f32[16,128]{1,0:T(8,128)S(1)} %get-tuple-element.17), channel_id=1, source_target_pairs={{0,16},{16,32},{32,48},{48,64},{64,80},{80,96},{96,112},{112,128},... | collective-permute-start | bytes 24584 | tf_op jit(solution)/shard_map/ppermute | solution.py:375
  27.9 5.1 %upper.1 = (f32[32,64,128]{2,1,0:T(8,128)}, f32[8,128,128]{2,1,0:T(8,128)S(1)}, f32[8,16,128]{2,1,0:T(8,128)S(1)}) custom-call(f32[2,64,16,128]{3,2,1,0:T(8,128)S(1)} %turn_late.1.tiles_ref, f32[16,16,128]{2,1,0:T(8,128)S(1)} %all-to-all-done.vectors_ref, f32[2,15,16,128]{3,2,1,0:T(8,128)S(1)} %after.1.after_ref, ...), custom_call_target="tpu_custom_call" | custom-call | tf_op jit(solution)/shard_map/upper/pallas_call | solution.py:328
  33.0 0.0 collective-permute-done.1.entering_ref
  33.0 1.4 %lower.1 = f32[32,64,128]{2,1,0:T(8,128)} custom-call(f32[8,128,128]{2,1,0:T(8,128)S(1)} %get-tuple-element.15.fixed_ref, f32[8,16,128]{2,1,0:T(8,128)S(1)} %get-tuple-element.16.response_ref, f32[16,128]{1,0:T(8,128)S(1)} %collective-permute-done.1.entering_ref, f32[32,64,128]{2,1,0:T(8,128)} %get-tuple-element.18.upper_ref), custom_call_target="tpu_custom_call", output_to_operand_aliasing={{}: (3, {})} | custom-call | tf_op jit(solution)/shard_map/lower/pallas_call | solution.py:361
  (1 shorter events, 0.0 us)
Async XLA Ops:
  0.0 0.7 %copy-start.2 = (f32[1,32,64]{2,1,0:T(8,128)S(1)}, f32[1,32,64]{2,1,0:T(8,128)}, u32[]{:S(2)}) copy-start(f32[1,32,64]{2,1,0:T(8,128)} %reflectors_ref.1) | copy-start | bytes 24580
  1.7 11.2 %copy-start = (f32[2048,128]{1,0:T(8,128)S(1)}, f32[2048,128]{1,0:T(8,128)}, u32[]{:S(2)}) copy-start(f32[2048,128]{1,0:T(8,128)} %rows_ref.3) | copy-start | bytes 3145732
  5.6 16.4 %all-to-all-start = ((f32[16,16,128]{2,1,0:T(8,128)}), f32[16,16,128]{2,1,0:T(8,128)S(1)}, u32[]{:S(2)}, u32[]{:S(2)}) async-start(f32[16,16,128]{2,1,0:T(8,128)} %pack.1), calls=%async_computation | async-start | bytes 262144 | tf_op jit(solution)/shard_map/all_to_all | solution.py:380
  12.9 5.9 %collective-permute-start = (f32[16,128]{1,0:T(8,128)S(1)}, f32[16,128]{1,0:T(8,128)S(1)}, u32[]{:S(2)}, u32[]{:S(2)}) collective-permute-start(f32[16,128]{1,0:T(8,128)S(1)} %slice.3), channel_id=1, source_target_pairs={{0,496},{16,0},{32,16},{48,32},{64,48},{80,64},{96,80},{112,96},{1... | collective-permute-start | bytes 24584 | tf_op jit(solution)/shard_map/ppermute | solution.py:375
  15.0 1.2 %copy-start.1 = (f32[2,64,16,128]{3,2,1,0:T(8,128)S(1)}, f32[2,64,16,128]{3,2,1,0:T(8,128)}, u32[]{:S(2)}) copy-start(f32[2,64,16,128]{3,2,1,0:T(8,128)} %turn_early.1.early_ref) | copy-start | bytes 3145732
  23.5 9.5 %collective-permute-start.1 = (f32[16,128]{1,0:T(8,128)S(1)}, f32[16,128]{1,0:T(8,128)S(1)}, u32[]{:S(2)}, u32[]{:S(2)}) collective-permute-start(f32[16,128]{1,0:T(8,128)S(1)} %get-tuple-element.17), channel_id=1, source_target_pairs={{0,16},{16,32},{32,48},{48,64},{64,80},{80,96},{96,112},{112,128},... | collective-permute-start | bytes 24584 | tf_op jit(solution)/shard_map/ppermute | solution.py:375

commit v5 on v4

v5 whole, which is shorter than its diff:
```python
import jax
import jax.numpy as jnp
from jax import lax
from jax.experimental import pallas as pl
from jax.experimental.pallas import tpu as pltpu
from jax.sharding import PartitionSpec as P

SWEEPS, BAND, HALF, LANES = 16, 64, 16, 128
TILE = (16, 128)
PARAMS = pltpu.CompilerParams(vmem_limit_bytes=8 * 2**20)


def lane_ids(shape=TILE):
    return lax.broadcasted_iota(jnp.int32, shape, len(shape) - 1)


def shear(tiles):
    slot = lane_ids(tiles[0].shape) // HALF
    for s in (1, 2, 4):
        moved = slot & s != 0
        tiles = [jnp.where(moved, tiles[(t - s) % 8], tiles[t]) for t in range(8)]
    return tiles


def swap_slots(tiles):
    tiles = shear([tiles[-t % 8] for t in range(8)])
    return shear([pltpu.roll(tiles[t], LANES - HALF * t, 1) if t else tiles[t] for t in range(8)])


def pack_kernel(reflectors_ref, copies_ref, turned_ref):
    vectors = reflectors_ref[0]
    first = lax.broadcasted_iota(jnp.int32, vectors.shape, 1) == 0
    vectors = jnp.where(first, jnp.ones_like(vectors), vectors)
    vectors = vectors * jnp.sqrt(2.0 / jnp.sum(vectors * vectors, axis=1, keepdims=True))
    padded = jnp.concatenate([vectors, jnp.zeros_like(vectors)], axis=1)
    padded = jnp.concatenate([padded] + [jnp.zeros_like(padded)] * 3, axis=0)
    turned_ref[...] = padded.T
    slot = lane_ids((8, LANES)) // HALF
    for half in range(2):
        packed = jnp.zeros((8, LANES), jnp.float32)
        for b in range(8):
            entries = turned_ref[pl.ds(b, 8, stride=8), :]
            entries = pltpu.roll(entries, (HALF * (b - half)) % LANES, 1)
            packed = jnp.where(slot == b, entries, packed)
        for sweep in range(SWEEPS):
            copies_ref[sweep, 8 * half : 8 * (half + 1), :] = packed


def pack(reflectors):
    return pl.pallas_call(
        pack_kernel,
        out_shape=jax.ShapeDtypeStruct((SWEEPS, 16, LANES), jnp.float32),
        scratch_shapes=[pltpu.VMEM((LANES, LANES), jnp.float32)],
        name="pack",
        compiler_params=PARAMS,
    )(reflectors)


def turn_kernel(rows_ref, tiles_ref, gathered_ref):
    for half in range(2):
        for o in range(8):
            for b in range(8):
                gathered_ref[half, o, HALF * b : HALF * (b + 1), :] = rows_ref[
                    pl.ds(half * HALF * BAND + 8 * o + b, HALF, stride=BAND), :
                ]
            turned = gathered_ref[half, o].T
            tiles = swap_slots([turned[HALF * g : HALF * (g + 1)] for g in range(8)])
            for b in range(8):
                tiles_ref[half, 8 * o + b] = tiles[b]


def turn(rows):
    return pl.pallas_call(
        turn_kernel,
        out_shape=jax.ShapeDtypeStruct((2, BAND) + TILE, jnp.float32),
        scratch_shapes=[pltpu.VMEM((2, 8, LANES, LANES), jnp.float32)],
        name="turn",
        compiler_params=PARAMS,
    )(rows)


def turn_back(turned, rows_ref, out_ref, half, o, sent):
    rows = turned.T
    for b in range(8):
        rows_ref[o, pl.ds(b, HALF, stride=8), :] = rows[HALF * b : HALF * (b + 1)]
    copy = pltpu.make_async_copy(
        rows_ref.at[o].reshape(HALF, 8, LANES),
        out_ref.at[pl.ds(HALF * half, HALF), pl.ds(8 * o, 8)],
        sent.at[o],
    )
    copy.start()
    return copy


def rows_after(state_ref):
    place = lane_ids() % HALF
    tile = jnp.zeros(TILE, jnp.float32)
    for i in range(SWEEPS - 1):
        tile = jnp.where(place == i, pltpu.roll(state_ref[BAND + i], (i - HALF + 1) % LANES, 1), tile)
    return tile


def spread(vectors_ref, half, sweep):
    packed = vectors_ref[sweep, 8 * half : 8 * (half + 1), :]
    return shear([pltpu.roll(packed, LANES - HALF * t, 1) if t else packed for t in range(8)])


def add_up(terms):
    while len(terms) > 1:
        terms = [sum(terms[t + 1 : t + 2], terms[t]) for t in range(0, len(terms), 2)]
    return terms[0]


def sweep_all(states, spreads, initial, entering, prepare, results):
    tiles = [state.shape[1:] for state in states]
    heads = [lane_ids(tile) % HALF == 0 for tile in tiles]
    halves = range(len(states))

    def entry(half, sweep, i):
        at = 8 * (i % 8) + i // 8
        return jnp.broadcast_to(spreads[half][sweep, at : at + 1, :], tiles[half])

    def before(half, sweep, i):
        return initial[half](i) if sweep == SWEEPS - 1 else states[half][i]

    def add(sums, i, term):
        sums[i % 2] = term if sums[i % 2] is None else sums[i % 2] + term

    if prepare:
        for sweep in range(SWEEPS - 1, SWEEPS - 4, -1):
            prepare(sweep)
    sums = [[None] * 2 for half in halves]
    for i in range(BAND):
        for half in halves:
            add(sums[half], i, entry(half, SWEEPS - 1, i) * initial[half](SWEEPS - 1 + i))
    totals = [add_up(terms) for terms in sums]
    for sweep in range(SWEEPS - 1, 0, -1):
        at = sweep + BAND - 1
        lasts = [before(half, sweep, at) - entry(half, sweep, BAND - 1) * totals[half] for half in halves]
        firsts = [
            jnp.where(heads[half], rows, pltpu.roll(lasts[half], 1, 1))
            for half, rows in enumerate(entering(sweep, lasts))
        ]
        for half in halves:
            states[half][at] = lasts[half]
            states[half][sweep - 1] = firsts[half]
        if prepare and sweep >= 3:
            prepare(sweep - 3)
        sums = [[None] * 2 for half in halves]
        for i in range(BAND - 1):
            for half in halves:
                row = before(half, sweep, sweep + i) - entry(half, sweep, i) * totals[half]
                states[half][sweep + i] = row
                add(sums[half], i, entry(half, sweep - 1, i + 1) * row)
        totals = [add_up(sums[half]) + entry(half, sweep - 1, 0) * firsts[half] for half in halves]
    for i in range(BAND):
        for half in halves:
            results[half][i] = states[half][i] - entry(half, 0, i) * totals[half]


def rows_of(tiles_ref, after_ref, half):
    return lambda i: tiles_ref[half, i] if i < BAND else after_ref[half, i - BAND]


def after_kernel(tiles_ref, halo_ref, after_ref, own_ref, gathered_ref):
    place, own_rows = lane_ids() % HALF, jnp.zeros(TILE, jnp.float32)
    for i in range(SWEEPS - 1):
        own_rows = jnp.where(place == i, pltpu.roll(tiles_ref[0, i], i, 1) if i else tiles_ref[0, 0], own_rows)
    own_ref[...] = own_rows
    last = lane_ids() % HALF == HALF - 1
    gathered_ref[...] = jnp.zeros_like(gathered_ref)
    gathered_ref[:HALF, :] = halo_ref[...]
    turned = gathered_ref[...].T
    slot = lane_ids() // HALF
    halo = turned[:HALF]
    for g in range(1, 8):
        halo = jnp.where(slot == g, pltpu.roll(turned[HALF * g : HALF * (g + 1)], HALF * g, 1), halo)
    for i in range(SWEEPS - 1):
        own = [pltpu.roll(tiles_ref[half, i], LANES - 1, 1) for half in range(2)]
        after_ref[0, i] = jnp.where(last, pltpu.roll(tiles_ref[1, i], HALF - 1, 1), own[0])
        after_ref[1, i] = jnp.where(last, pltpu.roll(halo, HALF - 1 - i, 1), own[1])


def rows_following(tiles, halo):
    return pl.pallas_call(
        after_kernel,
        out_shape=(
            jax.ShapeDtypeStruct((2, SWEEPS - 1) + TILE, jnp.float32),
            jax.ShapeDtypeStruct(TILE, jnp.float32),
        ),
        scratch_shapes=[pltpu.VMEM((LANES, LANES), jnp.float32)],
        name="after",
        compiler_params=PARAMS,
    )(tiles, halo)


def with_units(rows):
    zeros = jnp.zeros((8, LANES), jnp.float32)
    return lambda i: jnp.concatenate([rows(i), zeros], axis=0)


def unit(sweep):
    i, wide = sweep - 1, (24, LANES)
    row, parity = lax.broadcasted_iota(jnp.int32, wide, 0), lane_ids(wide) // HALF % 2
    return jnp.where(jnp.logical_and(row == 16 + i % 8, parity == i // 8), 1.0, 0.0)


def leave_kernel(
    tiles_ref, vectors_ref, after_ref,
    leaving_ref, lower_done_ref, upper_done_ref,
    lower_ref, upper_ref, lower_spread_ref, upper_spread_ref,
):
    rows = [rows_of(tiles_ref, after_ref, half) for half in range(2)]
    spreads = lower_spread_ref, upper_spread_ref

    def prepare(sweep):
        for half in range(2):
            for b, tile in enumerate(spread(vectors_ref, half, sweep)):
                spreads[half][sweep, 8 * b : 8 * (b + 1), :] = tile

    sweep_all(
        (lower_ref, upper_ref),
        spreads,
        (with_units(rows[0]), rows[1]),
        lambda sweep, lasts: (unit(sweep), pltpu.roll(lasts[0][:16], LANES - HALF + 1, 1)),
        prepare,
        (lower_done_ref, upper_done_ref),
    )
    leaving_ref[...] = rows_after(upper_ref)


STATE, WIDE, SPREAD = (BAND + SWEEPS,) + TILE, (BAND + SWEEPS, 24, LANES), (SWEEPS, BAND, LANES)
OCTS = (8, LANES, LANES)
OUT = (2 * HALF, BAND, LANES)
VMEM, ANY = pl.BlockSpec(memory_space=pltpu.VMEM), pl.BlockSpec(memory_space=pl.ANY)


def leave(tiles, vectors, after):
    shapes = TILE, (BAND, 24, LANES), (BAND,) + TILE
    return pl.pallas_call(
        leave_kernel,
        out_shape=tuple(jax.ShapeDtypeStruct(shape, jnp.float32) for shape in shapes),
        scratch_shapes=[pltpu.VMEM(shape, jnp.float32) for shape in (WIDE, STATE, SPREAD, SPREAD)],
        name="leave",
        compiler_params=PARAMS,
    )(tiles, vectors, after)


def upper_kernel(lower_ref, upper_ref, out_ref, fixed_ref, response_ref, rows_ref, sent):
    copies = []
    for o in range(8):
        turned = jnp.concatenate(swap_slots([upper_ref[8 * o + b] for b in range(8)]), axis=0)
        copies.append(turn_back(turned, rows_ref, out_ref, 1, o, sent))
    slot = lane_ids((8, LANES)) // HALF
    for o in range(8):
        fixed_ref[o] = jnp.concatenate(swap_slots([lower_ref[8 * o + b, :16, :] for b in range(8)]), axis=0)
        first, second = None, None
        for b in range(8):
            one = lower_ref[8 * o + b, 16:, :]
            parts = one, pltpu.roll(one, HALF, 1)
            first = parts[0] if first is None else jnp.where(slot == b, parts[b % 2], first)
            second = parts[1] if second is None else jnp.where(slot == b, parts[1 - b % 2], second)
        response_ref[o, :8, :] = first
        response_ref[o, 8:, :] = second
    for copy in copies:
        copy.wait()


def upper(*operands):
    return pl.pallas_call(
        upper_kernel,
        out_shape=tuple(jax.ShapeDtypeStruct(shape, jnp.float32) for shape in (OUT, OCTS, (8,) + TILE)),
        out_specs=(ANY, VMEM, VMEM),
        scratch_shapes=[pltpu.VMEM(OCTS, jnp.float32), pltpu.SemaphoreType.DMA((8,))],
        name="upper",
        compiler_params=PARAMS,
    )(*operands)


def lower_kernel(fixed_ref, response_ref, entering_ref, own_ref, upper_ref, out_ref, rows_ref, sent):
    tile = jnp.where(lax.axis_index("row") == 0, own_ref[...], entering_ref[...])
    entering = jnp.concatenate(
        [tile] + [pltpu.roll(tile, LANES - HALF * g, 1) for g in range(1, 8)], axis=0
    )[:, :HALF]
    copies = []
    for o in range(8):
        added = lax.dot_general(
            entering,
            response_ref[o],
            (((1,), (0,)), ((), ())),
            precision=lax.Precision.HIGHEST,
            preferred_element_type=jnp.float32,
        )
        copies.append(turn_back(fixed_ref[o] + added, rows_ref, out_ref, 0, o, sent))
    for copy in copies:
        copy.wait()


def lower(fixed, response, entering, own, upper_rows):
    return pl.pallas_call(
        lower_kernel,
        out_shape=jax.ShapeDtypeStruct(OUT, jnp.float32),
        in_specs=[VMEM] * 4 + [ANY],
        out_specs=ANY,
        scratch_shapes=[pltpu.VMEM(OCTS, jnp.float32), pltpu.SemaphoreType.DMA((8,))],
        input_output_aliases={4: 0},
        name="lower",
        compiler_params=PARAMS,
    )(fixed, response, entering, own, upper_rows)


def neighbour(value, step):
    owners = range(lax.axis_size("row"))
    return lax.ppermute(value, "row", [(i, i + step) for i in owners if i + step in owners])


def local(eigvecs, reflectors):
    vectors = lax.all_to_all(pack(reflectors), "col", 0, 0, tiled=True)
    halo = neighbour(eigvecs[:SWEEPS], -1)
    return sweeps(eigvecs, halo, vectors)


def sweeps(eigvecs, halo, vectors):
    tiles = turn(eigvecs)
    after, own = rows_following(tiles, halo)
    leaving, *done = leave(tiles, vectors, after)
    entering = neighbour(leaving, 1)
    upper_rows, fixed, response = upper(*done)
    return lower(fixed, response, entering, own, upper_rows).reshape(eigvecs.shape)


def solution(mesh):
    return jax.shard_map(
        local,
        mesh=mesh,
        in_specs=(P("row", "col"), P("col", "row", None)),
        out_specs=P("row", "col"),
        check_vma=False,
    )
```

time: 34.8 us -> 33.9 us (0.974)
  the two profiles are of different devices: /device:TPU:27 before, /device:TPU:6 now
where the time goes in v5:
time: 33.9 us; the launch traced here: 33.5 us
  starting transfers between devices  19.4 us (57%)
  Pallas kernels  8.22 us (24%)
  waiting for transfers between devices  3.17 us (9%)
  local copies, waits for them, and re-layouts  2.64 us (8%)
    all_to_all x1, starting transfers between devices, local(): vectors = lax.all_to_all(pack(reflectors), 'col', 0, 0, tiled=True)  10.4 us
    ppermute x2, starting transfers between devices, neighbour(): lax.ppermute(value, 'row', [(i, i + step) for i in owners if i + step in...  9.01 us
    pallas_call x1, Pallas kernels, leave(): pl.pallas_call(leave_kernel, out_shape=tuple((jax.ShapeDtypeStruct(shape,...  3.5 us
    ppermute x2, waiting for transfers between devices, neighbour(): lax.ppermute(value, 'row', [(i, i + step) for i in owners if i + step in...  3.17 us
    unnamed x4, local copies, waits for them, and re-layouts  1.94 us
    pallas_call x1, Pallas kernels, lower(): pl.pallas_call(lower_kernel, out_shape=jax.ShapeDtypeStruct(OUT, jnp.floa...  1.43 us
    pallas_call x1, Pallas kernels, upper(): pl.pallas_call(upper_kernel, out_shape=tuple((jax.ShapeDtypeStruct(shape,...  1.1 us
    pallas_call x1, Pallas kernels, pack(): pl.pallas_call(pack_kernel, out_shape=jax.ShapeDtypeStruct((SWEEPS, 16, L...  0.94 us
  transfers between devices with their start and end apart: 3, of which 1 were waited for; matrix products, arithmetic and copies ran while one was open for 2% of the time, Pallas kernels for 7%

profile of v5, /device:TPU:6, one launch (start us, length us, event | category | flops | bytes accessed | tf_op | source)
XLA Modules:
  0.0 33.5 jit_solution(4223606750990972375)
XLA Ops:
  0.0 0.0 copy-start.1
  0.0 0.7 %copy-done.1 = f32[1,32,64]{2,1,0:T(8,128)S(1)} copy-done((f32[1,32,64]{2,1,0:T(8,128)S(1)}, f32[1,32,64]{2,1,0:T(8,128)}, u32[]{:S(2)}) %copy-start.1) | copy-done | bytes 8216
  0.7 0.9 %pack.1 = f32[16,16,128]{2,1,0:T(8,128)} custom-call(f32[1,32,64]{2,1,0:T(8,128)S(1)} %copy-done.1), custom_call_target="tpu_custom_call" | custom-call | tf_op jit(solution)/shard_map/pack/pallas_call | solution.py:50
  1.7 10.4 %all-to-all-start = ((f32[16,16,128]{2,1,0:T(8,128)}), f32[16,16,128]{2,1,0:T(8,128)S(1)}, u32[]{:S(2)}, u32[]{:S(2)}) async-start(f32[16,16,128]{2,1,0:T(8,128)} %pack.1), calls=%async_computation | async-start | bytes 262144 | tf_op jit(solution)/shard_map/all_to_all | solution.py:318
  12.1 0.7 %slice.3 = f32[16,128]{1,0:T(8,128)S(1)} slice(f32[2048,128]{1,0:T(8,128)} %rows_ref.1), slice={[0:16], [0:128]} | slice | bytes 16384 | tf_op jit(solution)/shard_map/slice | solution.py:319
  12.8 5.6 %collective-permute-start = (f32[16,128]{1,0:T(8,128)S(1)}, f32[16,128]{1,0:T(8,128)S(1)}, u32[]{:S(2)}, u32[]{:S(2)}) collective-permute-start(f32[16,128]{1,0:T(8,128)S(1)} %slice.3), channel_id=1, source_target_pairs={{16,0},{32,16},{48,32},{64,48},{80,64},{96,80},{112,96},{128,112},... | collective-permute-start | bytes 24584 | tf_op jit(solution)/shard_map/ppermute | solution.py:314
  18.4 0.0 copy-start
  18.4 1.2 %copy-done = f32[2048,128]{1,0:T(8,128)S(1)} copy-done((f32[2048,128]{1,0:T(8,128)S(1)}, f32[2048,128]{1,0:T(8,128)}, u32[]{:S(2)}) %copy-start) | copy-done | bytes 1048600
  19.7 0.9 %turn.1.tiles_ref = f32[2,64,16,128]{3,2,1,0:T(8,128)S(1)} custom-call(f32[2048,128]{1,0:T(8,128)S(1)} %copy-done), custom_call_target="tpu_custom_call" | custom-call | tf_op jit(solution)/shard_map/turn/pallas_call | solution.py:73
  20.6 0.0 collective-permute-done.halo_ref
  20.6 0.3 after.1
  20.9 0.0 all-to-all-done.vectors_ref
  20.9 3.5 %leave.1 = (f32[16,128]{1,0:T(8,128)S(1)}, f32[64,24,128]{2,1,0:T(8,128)S(1)}, f32[64,16,128]{2,1,0:T(8,128)S(1)}) custom-call(f32[2,64,16,128]{3,2,1,0:T(8,128)S(1)} %turn.1.tiles_ref, f32[16,16,128]{2,1,0:T(8,128)S(1)} %all-to-all-done.vectors_ref, f32[2,15,16,128]{3,2,1,0:T(8,128)S(1)} %get-tuple-element.13.after_ref), custom_call_target="tpu_custom_call" | custom-call | tf_op jit(solution)/shard_map/leave/pallas_call | solution.py:240
  24.4 3.4 %collective-permute-start.1 = (f32[16,128]{1,0:T(8,128)S(1)}, f32[16,128]{1,0:T(8,128)S(1)}, u32[]{:S(2)}, u32[]{:S(2)}) collective-permute-start(f32[16,128]{1,0:T(8,128)S(1)} %get-tuple-element.18), channel_id=1, source_target_pairs={{0,16},{16,32},{32,48},{48,64},{64,80},{80,96},{96,112},{112,128},... | collective-permute-start | bytes 24584 | tf_op jit(solution)/shard_map/ppermute | solution.py:314
  27.8 1.1 %upper.1 = (f32[32,64,128]{2,1,0:T(8,128)}, f32[8,128,128]{2,1,0:T(8,128)S(1)}, f32[8,16,128]{2,1,0:T(8,128)S(1)}) custom-call(f32[64,24,128]{2,1,0:T(8,128)S(1)} %get-tuple-element.14.lower_ref, f32[64,16,128]{2,1,0:T(8,128)S(1)} %get-tuple-element.15.upper_ref), custom_call_target="tpu_custom_call" | custom-call | tf_op jit(solution)/shard_map/upper/pallas_call | solution.py:270
  28.9 3.2 %collective-permute-done.1.entering_ref = f32[16,128]{1,0:T(8,128)S(1)} collective-permute-done((f32[16,128]{1,0:T(8,128)S(1)}, f32[16,128]{1,0:T(8,128)S(1)}, u32[]{:S(2)}, u32[]{:S(2)}) %collective-permute-start.1) | collective-permute-done | bytes 8224 | tf_op jit(solution)/shard_map/ppermute | solution.py:314
  32.1 1.4 %lower.1 = f32[32,64,128]{2,1,0:T(8,128)} custom-call(f32[8,128,128]{2,1,0:T(8,128)S(1)} %get-tuple-element.16.fixed_ref, f32[8,16,128]{2,1,0:T(8,128)S(1)} %get-tuple-element.17.response_ref, f32[16,128]{1,0:T(8,128)S(1)} %collective-permute-done.1.entering_ref, f32[16,128]{1,0:T(8,128)S(1)} %get-tuple-element.19.own_ref, ...), custom_call_target="tpu_custom_call", output_to_operand_aliasing={{}: (4, {})} | custom-call | tf_op jit(solution)/shard_map/lower/pallas_call | solution.py:300
Async XLA Ops:
  0.0 0.7 %copy-start.1 = (f32[1,32,64]{2,1,0:T(8,128)S(1)}, f32[1,32,64]{2,1,0:T(8,128)}, u32[]{:S(2)}) copy-start(f32[1,32,64]{2,1,0:T(8,128)} %reflectors_ref.1) | copy-start | bytes 24580
  1.7 19.3 %all-to-all-start = ((f32[16,16,128]{2,1,0:T(8,128)}), f32[16,16,128]{2,1,0:T(8,128)S(1)}, u32[]{:S(2)}, u32[]{:S(2)}) async-start(f32[16,16,128]{2,1,0:T(8,128)} %pack.1), calls=%async_computation | async-start | bytes 262144 | tf_op jit(solution)/shard_map/all_to_all | solution.py:318
  12.8 7.8 %collective-permute-start = (f32[16,128]{1,0:T(8,128)S(1)}, f32[16,128]{1,0:T(8,128)S(1)}, u32[]{:S(2)}, u32[]{:S(2)}) collective-permute-start(f32[16,128]{1,0:T(8,128)S(1)} %slice.3), channel_id=1, source_target_pairs={{16,0},{32,16},{48,32},{64,48},{80,64},{96,80},{112,96},{128,112},... | collective-permute-start | bytes 24584 | tf_op jit(solution)/shard_map/ppermute | solution.py:314
  18.4 1.2 %copy-start = (f32[2048,128]{1,0:T(8,128)S(1)}, f32[2048,128]{1,0:T(8,128)}, u32[]{:S(2)}) copy-start(f32[2048,128]{1,0:T(8,128)} %rows_ref.1) | copy-start | bytes 3145732
  24.4 7.7 %collective-permute-start.1 = (f32[16,128]{1,0:T(8,128)S(1)}, f32[16,128]{1,0:T(8,128)S(1)}, u32[]{:S(2)}, u32[]{:S(2)}) collective-permute-start(f32[16,128]{1,0:T(8,128)S(1)} %get-tuple-element.18), channel_id=1, source_target_pairs={{0,16},{16,32},{32,48},{48,64},{64,80},{80,96},{96,112},{112,128},... | collective-permute-start | bytes 24584 | tf_op jit(solution)/shard_map/ppermute | solution.py:314

commit v6 on v5

--- a/solution.py
+++ b/solution.py
@@ -111,7 +111,7 @@
     return terms[0]
 
 
-def sweep_all(states, spreads, initial, entering, prepare, results):
+def sweep_all(states, spreads, initial, entering, prepare, results, ways=2):
     tiles = [state.shape[1:] for state in states]
     heads = [lane_ids(tile) % HALF == 0 for tile in tiles]
     halves = range(len(states))
@@ -124,12 +124,12 @@
         return initial[half](i) if sweep == SWEEPS - 1 else states[half][i]
 
     def add(sums, i, term):
-        sums[i % 2] = term if sums[i % 2] is None else sums[i % 2] + term
+        sums[i % ways] = term if sums[i % ways] is None else sums[i % ways] + term
 
     if prepare:
         for sweep in range(SWEEPS - 1, SWEEPS - 4, -1):
             prepare(sweep)
-    sums = [[None] * 2 for half in halves]
+    sums = [[None] * ways for half in halves]
     for i in range(BAND):
         for half in halves:
             add(sums[half], i, entry(half, SWEEPS - 1, i) * initial[half](SWEEPS - 1 + i))
@@ -146,7 +146,7 @@
             states[half][sweep - 1] = firsts[half]
         if prepare and sweep >= 3:
             prepare(sweep - 3)
-        sums = [[None] * 2 for half in halves]
+        sums = [[None] * ways for half in halves]
         for i in range(BAND - 1):
             for half in halves:
                 row = before(half, sweep, sweep + i) - entry(half, sweep, i) * totals[half]
@@ -194,22 +194,12 @@
     )(tiles, halo)
 
 
-def with_units(rows):
-    zeros = jnp.zeros((8, LANES), jnp.float32)
-    return lambda i: jnp.concatenate([rows(i), zeros], axis=0)
-
-
-def unit(sweep):
-    i, wide = sweep - 1, (24, LANES)
-    row, parity = lax.broadcasted_iota(jnp.int32, wide, 0), lane_ids(wide) // HALF % 2
-    return jnp.where(jnp.logical_and(row == 16 + i % 8, parity == i // 8), 1.0, 0.0)
-
-
 def leave_kernel(
     tiles_ref, vectors_ref, after_ref,
-    leaving_ref, lower_done_ref, upper_done_ref,
+    leaving_ref, lower_done_ref, upper_done_ref, spread_done_ref,
     lower_ref, upper_ref, lower_spread_ref, upper_spread_ref,
 ):
+    zeros = jnp.zeros(TILE, jnp.float32)
     rows = [rows_of(tiles_ref, after_ref, half) for half in range(2)]
     spreads = lower_spread_ref, upper_spread_ref
 
@@ -217,12 +207,14 @@
         for half in range(2):
             for b, tile in enumerate(spread(vectors_ref, half, sweep)):
                 spreads[half][sweep, 8 * b : 8 * (b + 1), :] = tile
+                if half == 0:
+                    spread_done_ref[sweep, 8 * b : 8 * (b + 1), :] = tile
 
     sweep_all(
         (lower_ref, upper_ref),
         spreads,
-        (with_units(rows[0]), rows[1]),
-        lambda sweep, lasts: (unit(sweep), pltpu.roll(lasts[0][:16], LANES - HALF + 1, 1)),
+        rows,
+        lambda sweep, lasts: (zeros, pltpu.roll(lasts[0], LANES - HALF + 1, 1)),
         prepare,
         (lower_done_ref, upper_done_ref),
     )
@@ -236,27 +228,45 @@
 
 
 def leave(tiles, vectors, after):
-    shapes = TILE, (BAND, 24, LANES), (BAND,) + TILE
+    shapes = TILE, (BAND,) + TILE, (BAND,) + TILE, SPREAD
     return pl.pallas_call(
         leave_kernel,
         out_shape=tuple(jax.ShapeDtypeStruct(shape, jnp.float32) for shape in shapes),
-        scratch_shapes=[pltpu.VMEM(shape, jnp.float32) for shape in (WIDE, STATE, SPREAD, SPREAD)],
+        scratch_shapes=[pltpu.VMEM(shape, jnp.float32) for shape in (STATE, STATE, SPREAD, SPREAD)],
         name="leave",
         compiler_params=PARAMS,
     )(tiles, vectors, after)
 
 
-def upper_kernel(lower_ref, upper_ref, out_ref, fixed_ref, response_ref, rows_ref, sent):
+def unit_sweeps(spread_ref, unit_ref, gaps):
+    tile = (8, LANES)
+    row, lane = lax.broadcasted_iota(jnp.int32, tile, 0), lane_ids(tile)
+    zeros = jnp.zeros(tile, jnp.float32)
+
+    def entering(sweep, lasts):
+        i = sweep - 1
+        gaps(sweep)
+        return (jnp.where(jnp.logical_and(row == i % 8, lane // HALF % 2 == i // 8), 1.0, 0.0),)
+
+    sweep_all((unit_ref,), (spread_ref,), (lambda i: zeros,), entering, None, (unit_ref,), 4)
+
+
+def upper_kernel(lower_ref, upper_ref, spread_ref, out_ref, fixed_ref, response_ref, rows_ref, sent, unit_ref):
     copies = []
-    for o in range(8):
-        turned = jnp.concatenate(swap_slots([upper_ref[8 * o + b] for b in range(8)]), axis=0)
-        copies.append(turn_back(turned, rows_ref, out_ref, 1, o, sent))
+
+    def gaps(sweep):
+        if sweep % 2:
+            o = 7 - sweep // 2
+            turned = jnp.concatenate(swap_slots([upper_ref[8 * o + b] for b in range(8)]), axis=0)
+            copies.append(turn_back(turned, rows_ref, out_ref, 1, o, sent))
+
+    unit_sweeps(spread_ref, unit_ref, gaps)
     slot = lane_ids((8, LANES)) // HALF
     for o in range(8):
-        fixed_ref[o] = jnp.concatenate(swap_slots([lower_ref[8 * o + b, :16, :] for b in range(8)]), axis=0)
+        fixed_ref[o] = jnp.concatenate(swap_slots([lower_ref[8 * o + b] for b in range(8)]), axis=0)
         first, second = None, None
         for b in range(8):
-            one = lower_ref[8 * o + b, 16:, :]
+            one = unit_ref[8 * o + b]
             parts = one, pltpu.roll(one, HALF, 1)
             first = parts[0] if first is None else jnp.where(slot == b, parts[b % 2], first)
             second = parts[1] if second is None else jnp.where(slot == b, parts[1 - b % 2], second)
@@ -271,10 +281,23 @@
         upper_kernel,
         out_shape=tuple(jax.ShapeDtypeStruct(shape, jnp.float32) for shape in (OUT, OCTS, (8,) + TILE)),
         out_specs=(ANY, VMEM, VMEM),
-        scratch_shapes=[pltpu.VMEM(OCTS, jnp.float32), pltpu.SemaphoreType.DMA((8,))],
+        scratch_shapes=[
+            pltpu.VMEM(OCTS, jnp.float32),
+            pltpu.SemaphoreType.DMA((8,)),
+            pltpu.VMEM((BAND + SWEEPS, 8, LANES), jnp.float32),
+        ],
         name="upper",
         compiler_params=PARAMS,
     )(*operands)
+
+
+def in_parts(values):
+    high = values.astype(jnp.bfloat16)
+    return high, (values - high.astype(jnp.float32)).astype(jnp.bfloat16)
+
+
+def product(a, b):
+    return jnp.dot(a, b, preferred_element_type=jnp.float32)
 
 
 def lower_kernel(fixed_ref, response_ref, entering_ref, own_ref, upper_ref, out_ref, rows_ref, sent):
@@ -282,15 +305,11 @@
     entering = jnp.concatenate(
         [tile] + [pltpu.roll(tile, LANES - HALF * g, 1) for g in range(1, 8)], axis=0
     )[:, :HALF]
+    entering_high, entering_low = in_parts(entering)
     copies = []
     for o in range(8):
-        added = lax.dot_general(
-            entering,
-            response_ref[o],
-            (((1,), (0,)), ((), ())),
-            precision=lax.Precision.HIGHEST,
-            preferred_element_type=jnp.float32,
-        )
+        high, low = in_parts(response_ref[o])
+        added = product(entering_high, high) + (product(entering_low, high) + product(entering_high, low))
         copies.append(turn_back(fixed_ref[o] + added, rows_ref, out_ref, 0, o, sent))
     for copy in copies:
         copy.wait()

time: 33.9 us -> 33.1 us (0.976)
  waiting for transfers between devices: 3.17 us -> 2.67 us
  Pallas kernels: 8.22 us -> 7.82 us
    pallas_call x1, Pallas kernels: 3.5 us -> 2.82 us  [leave(): pl.pallas_call(leave_kernel, out_shape=tuple((jax.ShapeDtypeStruct(shape,...]
    pallas_call x1, Pallas kernels: 1.1 us -> 1.59 us  [upper(): pl.pallas_call(upper_kernel, out_shape=tuple((jax.ShapeDtypeStruct(shape,...]
    ppermute x2, waiting for transfers between devices: 3.17 us -> 2.67 us  [neighbour(): lax.ppermute(value, 'row', [(i, i + step) for i in owners if i + step in...]
  transfers between devices with their start and end apart: 3 -> 3, of which waited for: 1 -> 1; matrix products, arithmetic and copies ran while one was open for 2% -> 2% of each run, Pallas kernels for 7% -> 9%
where the time goes in v6:
time: 33.1 us; the launch traced here: 32.6 us
  starting transfers between devices  19.4 us (59%)
  Pallas kernels  7.82 us (24%)
  waiting for transfers between devices  2.67 us (8%)
  local copies, waits for them, and re-layouts  2.64 us (8%)
    all_to_all x1, starting transfers between devices, local(): vectors = lax.all_to_all(pack(reflectors), 'col', 0, 0, tiled=True)  10.4 us
    ppermute x2, starting transfers between devices, neighbour(): lax.ppermute(value, 'row', [(i, i + step) for i in owners if i + step in...  9.01 us
    pallas_call x1, Pallas kernels, leave(): pl.pallas_call(leave_kernel, out_shape=tuple((jax.ShapeDtypeStruct(shape,...  2.82 us
    ppermute x2, waiting for transfers between devices, neighbour(): lax.ppermute(value, 'row', [(i, i + step) for i in owners if i + step in...  2.67 us
    unnamed x4, local copies, waits for them, and re-layouts  1.94 us
    pallas_call x1, Pallas kernels, upper(): pl.pallas_call(upper_kernel, out_shape=tuple((jax.ShapeDtypeStruct(shape,...  1.59 us
    pallas_call x1, Pallas kernels, lower(): pl.pallas_call(lower_kernel, out_shape=jax.ShapeDtypeStruct(OUT, jnp.floa...  1.22 us
    pallas_call x1, Pallas kernels, pack(): pl.pallas_call(pack_kernel, out_shape=jax.ShapeDtypeStruct((SWEEPS, 16, L...  0.94 us
  transfers between devices with their start and end apart: 3, of which 1 were waited for; matrix products, arithmetic and copies ran while one was open for 2% of the time, Pallas kernels for 9%

profile of v6, /device:TPU:6, one launch (start us, length us, event | category | flops | bytes accessed | tf_op | source)
XLA Modules:
  0.0 32.6 jit_solution(10586254092852453394)
XLA Ops:
  0.0 0.0 copy-start.1
  0.0 0.7 %copy-done.1 = f32[1,32,64]{2,1,0:T(8,128)S(1)} copy-done((f32[1,32,64]{2,1,0:T(8,128)S(1)}, f32[1,32,64]{2,1,0:T(8,128)}, u32[]{:S(2)}) %copy-start.1) | copy-done | bytes 8216
  0.7 0.9 %pack.1 = f32[16,16,128]{2,1,0:T(8,128)} custom-call(f32[1,32,64]{2,1,0:T(8,128)S(1)} %copy-done.1), custom_call_target="tpu_custom_call" | custom-call | tf_op jit(solution)/shard_map/pack/pallas_call | solution.py:50
  1.7 10.4 %all-to-all-start = ((f32[16,16,128]{2,1,0:T(8,128)}), f32[16,16,128]{2,1,0:T(8,128)S(1)}, u32[]{:S(2)}, u32[]{:S(2)}) async-start(f32[16,16,128]{2,1,0:T(8,128)} %pack.1), calls=%async_computation | async-start | bytes 262144 | tf_op jit(solution)/shard_map/all_to_all | solution.py:337
  12.1 0.7 %slice.3 = f32[16,128]{1,0:T(8,128)S(1)} slice(f32[2048,128]{1,0:T(8,128)} %rows_ref.1), slice={[0:16], [0:128]} | slice | bytes 16384 | tf_op jit(solution)/shard_map/slice | solution.py:338
  12.8 5.6 %collective-permute-start = (f32[16,128]{1,0:T(8,128)S(1)}, f32[16,128]{1,0:T(8,128)S(1)}, u32[]{:S(2)}, u32[]{:S(2)}) collective-permute-start(f32[16,128]{1,0:T(8,128)S(1)} %slice.3), channel_id=1, source_target_pairs={{16,0},{32,16},{48,32},{64,48},{80,64},{96,80},{112,96},{128,112},... | collective-permute-start | bytes 24584 | tf_op jit(solution)/shard_map/ppermute | solution.py:333
  18.4 0.0 copy-start
  18.4 1.2 %copy-done = f32[2048,128]{1,0:T(8,128)S(1)} copy-done((f32[2048,128]{1,0:T(8,128)S(1)}, f32[2048,128]{1,0:T(8,128)}, u32[]{:S(2)}) %copy-start) | copy-done | bytes 1048600
  19.7 0.9 %turn.1.tiles_ref = f32[2,64,16,128]{3,2,1,0:T(8,128)S(1)} custom-call(f32[2048,128]{1,0:T(8,128)S(1)} %copy-done), custom_call_target="tpu_custom_call" | custom-call | tf_op jit(solution)/shard_map/turn/pallas_call | solution.py:73
  20.6 0.0 collective-permute-done.halo_ref
  20.6 0.3 after.1
  20.9 0.0 all-to-all-done.vectors_ref
  20.9 2.8 %leave.1 = (f32[16,128]{1,0:T(8,128)S(1)}, f32[64,16,128]{2,1,0:T(8,128)S(1)}, f32[64,16,128]{2,1,0:T(8,128)S(1)}, f32[16,64,128]{2,1,0:T(8,128)S(1)}) custom-call(f32[2,64,16,128]{3,2,1,0:T(8,128)S(1)} %turn.1.tiles_ref, f32[16,16,128]{2,1,0:T(8,128)S(1)} %all-to-all-done.vectors_ref, f32[2,15,16,128]{3,2,1,0:T(8,128)S(1)} %get-tuple-element.14.after_ref), custom_call_target="tpu_custom_call" | custom-call | tf_op jit(solution)/shard_map/leave/pallas_call | solution.py:232
  23.8 3.4 %collective-permute-start.1 = (f32[16,128]{1,0:T(8,128)S(1)}, f32[16,128]{1,0:T(8,128)S(1)}, u32[]{:S(2)}, u32[]{:S(2)}) collective-permute-start(f32[16,128]{1,0:T(8,128)S(1)} %get-tuple-element.20), channel_id=1, source_target_pairs={{0,16},{16,32},{32,48},{48,64},{64,80},{80,96},{96,112},{112,128},... | collective-permute-start | bytes 24584 | tf_op jit(solution)/shard_map/ppermute | solution.py:333
  27.1 1.6 %upper.1 = (f32[32,64,128]{2,1,0:T(8,128)}, f32[8,128,128]{2,1,0:T(8,128)S(1)}, f32[8,16,128]{2,1,0:T(8,128)S(1)}) custom-call(f32[64,16,128]{2,1,0:T(8,128)S(1)} %get-tuple-element.15.lower_ref, f32[64,16,128]{2,1,0:T(8,128)S(1)} %get-tuple-element.16.upper_ref, f32[16,64,128]{2,1,0:T(8,128)S(1)} %get-tuple-element.17.spread_ref), custom_call_target="tpu_custom_call" | custom-call | tf_op jit(solution)/shard_map/upper/pallas_call | solution.py:280
  28.8 2.7 %collective-permute-done.1.entering_ref = f32[16,128]{1,0:T(8,128)S(1)} collective-permute-done((f32[16,128]{1,0:T(8,128)S(1)}, f32[16,128]{1,0:T(8,128)S(1)}, u32[]{:S(2)}, u32[]{:S(2)}) %collective-permute-start.1) | collective-permute-done | bytes 8224 | tf_op jit(solution)/shard_map/ppermute | solution.py:333
  31.4 1.2 %lower.1 = f32[32,64,128]{2,1,0:T(8,128)} custom-call(f32[8,128,128]{2,1,0:T(8,128)S(1)} %get-tuple-element.18.fixed_ref, f32[8,16,128]{2,1,0:T(8,128)S(1)} %get-tuple-element.19.response_ref, f32[16,128]{1,0:T(8,128)S(1)} %collective-permute-done.1.entering_ref, f32[16,128]{1,0:T(8,128)S(1)} %get-tuple-element.21.own_ref, ...), custom_call_target="tpu_custom_call", output_to_operand_aliasing={{}: (4, {})} | custom-call | tf_op jit(solution)/shard_map/lower/pallas_call | solution.py:319
Async XLA Ops:
  0.0 0.7 %copy-start.1 = (f32[1,32,64]{2,1,0:T(8,128)S(1)}, f32[1,32,64]{2,1,0:T(8,128)}, u32[]{:S(2)}) copy-start(f32[1,32,64]{2,1,0:T(8,128)} %reflectors_ref.1) | copy-start | bytes 24580
  1.7 19.3 %all-to-all-start = ((f32[16,16,128]{2,1,0:T(8,128)}), f32[16,16,128]{2,1,0:T(8,128)S(1)}, u32[]{:S(2)}, u32[]{:S(2)}) async-start(f32[16,16,128]{2,1,0:T(8,128)} %pack.1), calls=%async_computation | async-start | bytes 262144 | tf_op jit(solution)/shard_map/all_to_all | solution.py:337
  12.8 7.8 %collective-permute-start = (f32[16,128]{1,0:T(8,128)S(1)}, f32[16,128]{1,0:T(8,128)S(1)}, u32[]{:S(2)}, u32[]{:S(2)}) collective-permute-start(f32[16,128]{1,0:T(8,128)S(1)} %slice.3), channel_id=1, source_target_pairs={{16,0},{32,16},{48,32},{64,48},{80,64},{96,80},{112,96},{128,112},... | collective-permute-start | bytes 24584 | tf_op jit(solution)/shard_map/ppermute | solution.py:333
  18.4 1.2 %copy-start = (f32[2048,128]{1,0:T(8,128)S(1)}, f32[2048,128]{1,0:T(8,128)}, u32[]{:S(2)}) copy-start(f32[2048,128]{1,0:T(8,128)} %rows_ref.1) | copy-start | bytes 3145732
  23.8 7.7 %collective-permute-start.1 = (f32[16,128]{1,0:T(8,128)S(1)}, f32[16,128]{1,0:T(8,128)S(1)}, u32[]{:S(2)}, u32[]{:S(2)}) collective-permute-start(f32[16,128]{1,0:T(8,128)S(1)} %get-tuple-element.20), channel_id=1, source_target_pairs={{0,16},{16,32},{32,48},{48,64},{64,80},{80,96},{96,112},{112,128},... | collective-permute-start | bytes 24584 | tf_op jit(solution)/shard_map/ppermute | solution.py:333

commit v7 on v6

--- a/solution.py
+++ b/solution.py
@@ -111,7 +111,7 @@
     return terms[0]
 
 
-def sweep_all(states, spreads, initial, entering, prepare, results, ways=2):
+def sweep_all(states, spreads, initial, entering, prepare, results, ways=2, final=0):
     tiles = [state.shape[1:] for state in states]
     heads = [lane_ids(tile) % HALF == 0 for tile in tiles]
     halves = range(len(states))
@@ -150,8 +150,15 @@
         for i in range(BAND - 1):
             for half in halves:
                 row = before(half, sweep, sweep + i) - entry(half, sweep, i) * totals[half]
+                if sweep == final:
+                    results[half][sweep + i] = row
+                    continue
                 states[half][sweep + i] = row
                 add(sums[half], i, entry(half, sweep - 1, i + 1) * row)
+        if sweep == final:
+            for half in halves:
+                results[half][0] = firsts[half]
+            return
         totals = [add_up(sums[half]) + entry(half, sweep - 1, 0) * firsts[half] for half in halves]
     for i in range(BAND):
         for half in halves:
@@ -217,6 +224,7 @@
         lambda sweep, lasts: (zeros, pltpu.roll(lasts[0], LANES - HALF + 1, 1)),
         prepare,
         (lower_done_ref, upper_done_ref),
+        final=1,
     )
     leaving_ref[...] = rows_after(upper_ref)
 
@@ -251,19 +259,41 @@
     sweep_all((unit_ref,), (spread_ref,), (lambda i: zeros,), entering, None, (unit_ref,), 4)
 
 
-def upper_kernel(lower_ref, upper_ref, spread_ref, out_ref, fixed_ref, response_ref, rows_ref, sent, unit_ref):
+def last_sweep(state_ref, entry):
+    sums = [None] * 4
+    for i in range(BAND):
+        term = entry(i) * state_ref[i]
+        sums[i % 4] = term if sums[i % 4] is None else sums[i % 4] + term
+    total = add_up(sums)
+    return lambda i: state_ref[i] - entry(i) * total
+
+
+def upper_kernel(
+    lower_ref, upper_ref, spread_ref, vectors_ref,
+    out_ref, fixed_ref, response_ref,
+    rows_ref, sent, unit_ref, last_ref,
+):
+    for b, tile in enumerate(spread(vectors_ref, 1, 0)):
+        last_ref[8 * b : 8 * (b + 1), :] = tile
+
+    def row_at(ref, i):
+        at = 8 * (i % 8) + i // 8
+        return jnp.broadcast_to(ref[at : at + 1, :], TILE)
+
+    upper_row = last_sweep(upper_ref, lambda i: row_at(last_ref, i))
+    lower_row = last_sweep(lower_ref, lambda i: row_at(spread_ref.at[0], i))
     copies = []
 
     def gaps(sweep):
         if sweep % 2:
             o = 7 - sweep // 2
-            turned = jnp.concatenate(swap_slots([upper_ref[8 * o + b] for b in range(8)]), axis=0)
+            turned = jnp.concatenate(swap_slots([upper_row(8 * o + b) for b in range(8)]), axis=0)
             copies.append(turn_back(turned, rows_ref, out_ref, 1, o, sent))
 
     unit_sweeps(spread_ref, unit_ref, gaps)
     slot = lane_ids((8, LANES)) // HALF
     for o in range(8):
-        fixed_ref[o] = jnp.concatenate(swap_slots([lower_ref[8 * o + b] for b in range(8)]), axis=0)
+        fixed_ref[o] = jnp.concatenate(swap_slots([lower_row(8 * o + b) for b in range(8)]), axis=0)
         first, second = None, None
         for b in range(8):
             one = unit_ref[8 * o + b]
@@ -285,6 +315,7 @@
             pltpu.VMEM(OCTS, jnp.float32),
             pltpu.SemaphoreType.DMA((8,)),
             pltpu.VMEM((BAND + SWEEPS, 8, LANES), jnp.float32),
+            pltpu.VMEM((BAND, LANES), jnp.float32),
         ],
         name="upper",
         compiler_params=PARAMS,
@@ -344,7 +375,7 @@
     after, own = rows_following(tiles, halo)
     leaving, *done = leave(tiles, vectors, after)
     entering = neighbour(leaving, 1)
-    upper_rows, fixed, response = upper(*done)
+    upper_rows, fixed, response = upper(*done, vectors)
     return lower(fixed, response, entering, own, upper_rows).reshape(eigvecs.shape)
 
 

time: 33.1 us -> 33 us (level)
  waiting for transfers between devices: 2.67 us -> 2.3 us
    pallas_call x1, Pallas kernels: 1.59 us -> 1.96 us  [upper(): pl.pallas_call(upper_kernel, out_shape=tuple((jax.ShapeDtypeStruct(shape,...]
    ppermute x2, waiting for transfers between devices: 2.67 us -> 2.3 us  [neighbour(): lax.ppermute(value, 'row', [(i, i + step) for i in owners if i + step in...]
  transfers between devices with their start and end apart: 3 -> 3, of which waited for: 1 -> 1; matrix products, arithmetic and copies ran while one was open for 2% -> 2% of each run, Pallas kernels for 9% -> 10%
where the time goes in v7:
time: 33 us; the launch traced here: 32.6 us
  starting transfers between devices  19.4 us (59%)
  Pallas kernels  8.11 us (25%)
  local copies, waits for them, and re-layouts  2.64 us (8%)
  waiting for transfers between devices  2.3 us (7%)
    all_to_all x1, starting transfers between devices, local(): vectors = lax.all_to_all(pack(reflectors), 'col', 0, 0, tiled=True)  10.4 us
    ppermute x2, starting transfers between devices, neighbour(): lax.ppermute(value, 'row', [(i, i + step) for i in owners if i + step in...  9.01 us
    pallas_call x1, Pallas kernels, leave(): pl.pallas_call(leave_kernel, out_shape=tuple((jax.ShapeDtypeStruct(shape,...  2.74 us
    ppermute x2, waiting for transfers between devices, neighbour(): lax.ppermute(value, 'row', [(i, i + step) for i in owners if i + step in...  2.3 us
    pallas_call x1, Pallas kernels, upper(): pl.pallas_call(upper_kernel, out_shape=tuple((jax.ShapeDtypeStruct(shape,...  1.96 us
    unnamed x4, local copies, waits for them, and re-layouts  1.94 us
    pallas_call x1, Pallas kernels, lower(): pl.pallas_call(lower_kernel, out_shape=jax.ShapeDtypeStruct(OUT, jnp.floa...  1.22 us
    pallas_call x1, Pallas kernels, pack(): pl.pallas_call(pack_kernel, out_shape=jax.ShapeDtypeStruct((SWEEPS, 16, L...  0.94 us
  transfers between devices with their start and end apart: 3, of which 1 were waited for; matrix products, arithmetic and copies ran while one was open for 2% of the time, Pallas kernels for 10%

profile of v7, /device:TPU:6, one launch (start us, length us, event | category | flops | bytes accessed | tf_op | source)
XLA Modules:
  0.0 32.6 jit_solution(7247420396769471739)
XLA Ops:
  0.0 0.0 copy-start.1
  0.0 0.7 %copy-done.1 = f32[1,32,64]{2,1,0:T(8,128)S(1)} copy-done((f32[1,32,64]{2,1,0:T(8,128)S(1)}, f32[1,32,64]{2,1,0:T(8,128)}, u32[]{:S(2)}) %copy-start.1) | copy-done | bytes 8216
  0.7 0.9 %pack.1 = f32[16,16,128]{2,1,0:T(8,128)} custom-call(f32[1,32,64]{2,1,0:T(8,128)S(1)} %copy-done.1), custom_call_target="tpu_custom_call" | custom-call | tf_op jit(solution)/shard_map/pack/pallas_call | solution.py:50
  1.7 10.4 %all-to-all-start = ((f32[16,16,128]{2,1,0:T(8,128)}), f32[16,16,128]{2,1,0:T(8,128)S(1)}, u32[]{:S(2)}, u32[]{:S(2)}) async-start(f32[16,16,128]{2,1,0:T(8,128)} %pack.1), calls=%async_computation | async-start | bytes 262144 | tf_op jit(solution)/shard_map/all_to_all | solution.py:368
  12.1 0.7 %slice.3 = f32[16,128]{1,0:T(8,128)S(1)} slice(f32[2048,128]{1,0:T(8,128)} %rows_ref.1), slice={[0:16], [0:128]} | slice | bytes 16384 | tf_op jit(solution)/shard_map/slice | solution.py:369
  12.8 5.6 %collective-permute-start = (f32[16,128]{1,0:T(8,128)S(1)}, f32[16,128]{1,0:T(8,128)S(1)}, u32[]{:S(2)}, u32[]{:S(2)}) collective-permute-start(f32[16,128]{1,0:T(8,128)S(1)} %slice.3), channel_id=1, source_target_pairs={{16,0},{32,16},{48,32},{64,48},{80,64},{96,80},{112,96},{128,112},... | collective-permute-start | bytes 24584 | tf_op jit(solution)/shard_map/ppermute | solution.py:364
  18.4 0.0 copy-start
  18.4 1.2 %copy-done = f32[2048,128]{1,0:T(8,128)S(1)} copy-done((f32[2048,128]{1,0:T(8,128)S(1)}, f32[2048,128]{1,0:T(8,128)}, u32[]{:S(2)}) %copy-start) | copy-done | bytes 1048600
  19.7 0.9 %turn.1.tiles_ref = f32[2,64,16,128]{3,2,1,0:T(8,128)S(1)} custom-call(f32[2048,128]{1,0:T(8,128)S(1)} %copy-done), custom_call_target="tpu_custom_call" | custom-call | tf_op jit(solution)/shard_map/turn/pallas_call | solution.py:73
  20.6 0.0 collective-permute-done.halo_ref
  20.6 0.3 after.1
  20.9 0.0 all-to-all-done.vectors_ref
  20.9 2.7 %leave.1 = (f32[16,128]{1,0:T(8,128)S(1)}, f32[64,16,128]{2,1,0:T(8,128)S(1)}, f32[64,16,128]{2,1,0:T(8,128)S(1)}, f32[16,64,128]{2,1,0:T(8,128)S(1)}) custom-call(f32[2,64,16,128]{3,2,1,0:T(8,128)S(1)} %turn.1.tiles_ref, f32[16,16,128]{2,1,0:T(8,128)S(1)} %all-to-all-done.vectors_ref, f32[2,15,16,128]{3,2,1,0:T(8,128)S(1)} %get-tuple-element.14.after_ref), custom_call_target="tpu_custom_call" | custom-call | tf_op jit(solution)/shard_map/leave/pallas_call | solution.py:240
  23.7 3.4 %collective-permute-start.1 = (f32[16,128]{1,0:T(8,128)S(1)}, f32[16,128]{1,0:T(8,128)S(1)}, u32[]{:S(2)}, u32[]{:S(2)}) collective-permute-start(f32[16,128]{1,0:T(8,128)S(1)} %get-tuple-element.20), channel_id=1, source_target_pairs={{0,16},{16,32},{32,48},{48,64},{64,80},{80,96},{96,112},{112,128},... | collective-permute-start | bytes 24584 | tf_op jit(solution)/shard_map/ppermute | solution.py:364
  27.1 2.0 %upper.1 = (f32[32,64,128]{2,1,0:T(8,128)}, f32[8,128,128]{2,1,0:T(8,128)S(1)}, f32[8,16,128]{2,1,0:T(8,128)S(1)}) custom-call(f32[64,16,128]{2,1,0:T(8,128)S(1)} %get-tuple-element.15.lower_ref, f32[64,16,128]{2,1,0:T(8,128)S(1)} %get-tuple-element.16.upper_ref, f32[16,64,128]{2,1,0:T(8,128)S(1)} %get-tuple-element.17.spread_ref, ...), custom_call_target="tpu_custom_call" | custom-call | tf_op jit(solution)/shard_map/upper/pallas_call | solution.py:310
  29.0 2.3 %collective-permute-done.1.entering_ref = f32[16,128]{1,0:T(8,128)S(1)} collective-permute-done((f32[16,128]{1,0:T(8,128)S(1)}, f32[16,128]{1,0:T(8,128)S(1)}, u32[]{:S(2)}, u32[]{:S(2)}) %collective-permute-start.1) | collective-permute-done | bytes 8224 | tf_op jit(solution)/shard_map/ppermute | solution.py:364
  31.3 1.2 %lower.1 = f32[32,64,128]{2,1,0:T(8,128)} custom-call(f32[8,128,128]{2,1,0:T(8,128)S(1)} %get-tuple-element.18.fixed_ref, f32[8,16,128]{2,1,0:T(8,128)S(1)} %get-tuple-element.19.response_ref, f32[16,128]{1,0:T(8,128)S(1)} %collective-permute-done.1.entering_ref, f32[16,128]{1,0:T(8,128)S(1)} %get-tuple-element.21.own_ref, ...), custom_call_target="tpu_custom_call", output_to_operand_aliasing={{}: (4, {})} | custom-call | tf_op jit(solution)/shard_map/lower/pallas_call | solution.py:350
Async XLA Ops:
  0.0 0.7 %copy-start.1 = (f32[1,32,64]{2,1,0:T(8,128)S(1)}, f32[1,32,64]{2,1,0:T(8,128)}, u32[]{:S(2)}) copy-start(f32[1,32,64]{2,1,0:T(8,128)} %reflectors_ref.1) | copy-start | bytes 24580
  1.7 19.3 %all-to-all-start = ((f32[16,16,128]{2,1,0:T(8,128)}), f32[16,16,128]{2,1,0:T(8,128)S(1)}, u32[]{:S(2)}, u32[]{:S(2)}) async-start(f32[16,16,128]{2,1,0:T(8,128)} %pack.1), calls=%async_computation | async-start | bytes 262144 | tf_op jit(solution)/shard_map/all_to_all | solution.py:368
  12.8 7.8 %collective-permute-start = (f32[16,128]{1,0:T(8,128)S(1)}, f32[16,128]{1,0:T(8,128)S(1)}, u32[]{:S(2)}, u32[]{:S(2)}) collective-permute-start(f32[16,128]{1,0:T(8,128)S(1)} %slice.3), channel_id=1, source_target_pairs={{16,0},{32,16},{48,32},{64,48},{80,64},{96,80},{112,96},{128,112},... | collective-permute-start | bytes 24584 | tf_op jit(solution)/shard_map/ppermute | solution.py:364
  18.4 1.2 %copy-start = (f32[2048,128]{1,0:T(8,128)S(1)}, f32[2048,128]{1,0:T(8,128)}, u32[]{:S(2)}) copy-start(f32[2048,128]{1,0:T(8,128)} %rows_ref.1) | copy-start | bytes 3145732
  23.7 7.7 %collective-permute-start.1 = (f32[16,128]{1,0:T(8,128)S(1)}, f32[16,128]{1,0:T(8,128)S(1)}, u32[]{:S(2)}, u32[]{:S(2)}) collective-permute-start(f32[16,128]{1,0:T(8,128)S(1)} %get-tuple-element.20), channel_id=1, source_target_pairs={{0,16},{16,32},{32,48},{48,64},{64,80},{80,96},{96,112},{112,128},... | collective-permute-start | bytes 24584 | tf_op jit(solution)/shard_map/ppermute | solution.py:364

commit v8 on v6

--- a/solution.py
+++ b/solution.py
@@ -52,7 +52,7 @@
         out_shape=jax.ShapeDtypeStruct((SWEEPS, 16, LANES), jnp.float32),
         scratch_shapes=[pltpu.VMEM((LANES, LANES), jnp.float32)],
         name="pack",
-        compiler_params=PARAMS,
+        compiler_params=pltpu.CompilerParams(vmem_limit_bytes=56 * 2**20),
     )(reflectors)
 
 

time: 33.1 us -> 33.1 us (level)
  Pallas kernels: 7.82 us -> 8.72 us
  local copies, waits for them, and re-layouts: 2.64 us -> 1.92 us
    unnamed x4 -> x2, local copies, waits for them, and re-layouts: 1.94 us -> 1.22 us
    pallas_call x1, Pallas kernels: 0.94 us -> 1.66 us  [pack(): pl.pallas_call(pack_kernel, out_shape=jax.ShapeDtypeStruct((SWEEPS, 16, L...]
where the time goes in v8:
time: 33.1 us; the launch traced here: 32.7 us
  starting transfers between devices  19.4 us (59%)
  Pallas kernels  8.72 us (26%)
  waiting for transfers between devices  2.57 us (8%)
  local copies, waits for them, and re-layouts  1.92 us (6%)
    all_to_all x1, starting transfers between devices, local(): vectors = lax.all_to_all(pack(reflectors), 'col', 0, 0, tiled=True)  10.4 us
    ppermute x2, starting transfers between devices, neighbour(): lax.ppermute(value, 'row', [(i, i + step) for i in owners if i + step in...  9.01 us
    pallas_call x1, Pallas kernels, leave(): pl.pallas_call(leave_kernel, out_shape=tuple((jax.ShapeDtypeStruct(shape,...  2.9 us
    ppermute x2, waiting for transfers between devices, neighbour(): lax.ppermute(value, 'row', [(i, i + step) for i in owners if i + step in...  2.57 us
    pallas_call x1, Pallas kernels, upper(): pl.pallas_call(upper_kernel, out_shape=tuple((jax.ShapeDtypeStruct(shape,...  1.7 us
    pallas_call x1, Pallas kernels, pack(): pl.pallas_call(pack_kernel, out_shape=jax.ShapeDtypeStruct((SWEEPS, 16, L...  1.66 us
    pallas_call x1, Pallas kernels, lower(): pl.pallas_call(lower_kernel, out_shape=jax.ShapeDtypeStruct(OUT, jnp.floa...  1.22 us
    unnamed x2, local copies, waits for them, and re-layouts  1.22 us
  transfers between devices with their start and end apart: 3, of which 1 were waited for; matrix products, arithmetic and copies ran while one was open for 2% of the time, Pallas kernels for 9%

profile of v8, /device:TPU:6, one launch (start us, length us, event | category | flops | bytes accessed | tf_op | source)
XLA Modules:
  0.0 32.7 jit_solution(10718098422032338204)
XLA Ops:
  0.0 1.7 %pack.1 = f32[16,16,128]{2,1,0:T(8,128)} custom-call(f32[1,32,64]{2,1,0:T(8,128)} %reflectors_ref.1), custom_call_target="tpu_custom_call" | custom-call | tf_op jit(solution)/shard_map/pack/pallas_call | solution.py:50
  1.7 10.4 %all-to-all-start = ((f32[16,16,128]{2,1,0:T(8,128)}), f32[16,16,128]{2,1,0:T(8,128)S(1)}, u32[]{:S(2)}, u32[]{:S(2)}) async-start(f32[16,16,128]{2,1,0:T(8,128)} %pack.1), calls=%async_computation | async-start | bytes 262144 | tf_op jit(solution)/shard_map/all_to_all | solution.py:337
  12.1 0.7 %slice.3 = f32[16,128]{1,0:T(8,128)S(1)} slice(f32[2048,128]{1,0:T(8,128)} %rows_ref.1), slice={[0:16], [0:128]} | slice | bytes 16384 | tf_op jit(solution)/shard_map/slice | solution.py:338
  12.8 5.6 %collective-permute-start = (f32[16,128]{1,0:T(8,128)S(1)}, f32[16,128]{1,0:T(8,128)S(1)}, u32[]{:S(2)}, u32[]{:S(2)}) collective-permute-start(f32[16,128]{1,0:T(8,128)S(1)} %slice.3), channel_id=1, source_target_pairs={{16,0},{32,16},{48,32},{64,48},{80,64},{96,80},{112,96},{128,112},... | collective-permute-start | bytes 24584 | tf_op jit(solution)/shard_map/ppermute | solution.py:333
  18.4 0.0 copy-start
  18.4 1.2 %copy-done = f32[2048,128]{1,0:T(8,128)S(1)} copy-done((f32[2048,128]{1,0:T(8,128)S(1)}, f32[2048,128]{1,0:T(8,128)}, u32[]{:S(2)}) %copy-start) | copy-done | bytes 1048600
  19.7 0.9 %turn.1.tiles_ref = f32[2,64,16,128]{3,2,1,0:T(8,128)S(1)} custom-call(f32[2048,128]{1,0:T(8,128)S(1)} %copy-done), custom_call_target="tpu_custom_call" | custom-call | tf_op jit(solution)/shard_map/turn/pallas_call | solution.py:73
  20.6 0.0 collective-permute-done.halo_ref
  20.6 0.3 after.1
  20.9 0.0 all-to-all-done.vectors_ref
  20.9 2.9 %leave.1 = (f32[16,128]{1,0:T(8,128)S(1)}, f32[64,16,128]{2,1,0:T(8,128)S(1)}, f32[64,16,128]{2,1,0:T(8,128)S(1)}, f32[16,64,128]{2,1,0:T(8,128)S(1)}) custom-call(f32[2,64,16,128]{3,2,1,0:T(8,128)S(1)} %turn.1.tiles_ref, f32[16,16,128]{2,1,0:T(8,128)S(1)} %all-to-all-done.vectors_ref, f32[2,15,16,128]{3,2,1,0:T(8,128)S(1)} %get-tuple-element.14.after_ref), custom_call_target="tpu_custom_call" | custom-call | tf_op jit(solution)/shard_map/leave/pallas_call | solution.py:232
  23.8 3.4 %collective-permute-start.1 = (f32[16,128]{1,0:T(8,128)S(1)}, f32[16,128]{1,0:T(8,128)S(1)}, u32[]{:S(2)}, u32[]{:S(2)}) collective-permute-start(f32[16,128]{1,0:T(8,128)S(1)} %get-tuple-element.20), channel_id=1, source_target_pairs={{0,16},{16,32},{32,48},{48,64},{64,80},{80,96},{96,112},{112,128},... | collective-permute-start | bytes 24584 | tf_op jit(solution)/shard_map/ppermute | solution.py:333
  27.2 1.7 %upper.1 = (f32[32,64,128]{2,1,0:T(8,128)}, f32[8,128,128]{2,1,0:T(8,128)S(1)}, f32[8,16,128]{2,1,0:T(8,128)S(1)}) custom-call(f32[64,16,128]{2,1,0:T(8,128)S(1)} %get-tuple-element.15.lower_ref, f32[64,16,128]{2,1,0:T(8,128)S(1)} %get-tuple-element.16.upper_ref, f32[16,64,128]{2,1,0:T(8,128)S(1)} %get-tuple-element.17.spread_ref), custom_call_target="tpu_custom_call" | custom-call | tf_op jit(solution)/shard_map/upper/pallas_call | solution.py:280
  28.9 2.6 %collective-permute-done.1.entering_ref = f32[16,128]{1,0:T(8,128)S(1)} collective-permute-done((f32[16,128]{1,0:T(8,128)S(1)}, f32[16,128]{1,0:T(8,128)S(1)}, u32[]{:S(2)}, u32[]{:S(2)}) %collective-permute-start.1) | collective-permute-done | bytes 8224 | tf_op jit(solution)/shard_map/ppermute | solution.py:333
  31.5 1.2 %lower.1 = f32[32,64,128]{2,1,0:T(8,128)} custom-call(f32[8,128,128]{2,1,0:T(8,128)S(1)} %get-tuple-element.18.fixed_ref, f32[8,16,128]{2,1,0:T(8,128)S(1)} %get-tuple-element.19.response_ref, f32[16,128]{1,0:T(8,128)S(1)} %collective-permute-done.1.entering_ref, f32[16,128]{1,0:T(8,128)S(1)} %get-tuple-element.21.own_ref, ...), custom_call_target="tpu_custom_call", output_to_operand_aliasing={{}: (4, {})} | custom-call | tf_op jit(solution)/shard_map/lower/pallas_call | solution.py:319
Async XLA Ops:
  1.7 19.3 %all-to-all-start = ((f32[16,16,128]{2,1,0:T(8,128)}), f32[16,16,128]{2,1,0:T(8,128)S(1)}, u32[]{:S(2)}, u32[]{:S(2)}) async-start(f32[16,16,128]{2,1,0:T(8,128)} %pack.1), calls=%async_computation | async-start | bytes 262144 | tf_op jit(solution)/shard_map/all_to_all | solution.py:337
  12.8 7.8 %collective-permute-start = (f32[16,128]{1,0:T(8,128)S(1)}, f32[16,128]{1,0:T(8,128)S(1)}, u32[]{:S(2)}, u32[]{:S(2)}) collective-permute-start(f32[16,128]{1,0:T(8,128)S(1)} %slice.3), channel_id=1, source_target_pairs={{16,0},{32,16},{48,32},{64,48},{80,64},{96,80},{112,96},{128,112},... | collective-permute-start | bytes 24584 | tf_op jit(solution)/shard_map/ppermute | solution.py:333
  18.4 1.2 %copy-start = (f32[2048,128]{1,0:T(8,128)S(1)}, f32[2048,128]{1,0:T(8,128)}, u32[]{:S(2)}) copy-start(f32[2048,128]{1,0:T(8,128)} %rows_ref.1) | copy-start | bytes 3145732
  23.8 7.7 %collective-permute-start.1 = (f32[16,128]{1,0:T(8,128)S(1)}, f32[16,128]{1,0:T(8,128)S(1)}, u32[]{:S(2)}, u32[]{:S(2)}) collective-permute-start(f32[16,128]{1,0:T(8,128)S(1)} %get-tuple-element.20), channel_id=1, source_target_pairs={{0,16},{16,32},{32,48},{48,64},{64,80},{80,96},{96,112},{112,128},... | collective-permute-start | bytes 24584 | tf_op jit(solution)/shard_map/ppermute | solution.py:333

commit v9 on v6

--- a/solution.py
+++ b/solution.py
@@ -210,12 +210,14 @@
                 if half == 0:
                     spread_done_ref[sweep, 8 * b : 8 * (b + 1), :] = tile
 
+    for sweep in range(SWEEPS - 1, -1, -1):
+        prepare(sweep)
     sweep_all(
         (lower_ref, upper_ref),
         spreads,
         rows,
         lambda sweep, lasts: (zeros, pltpu.roll(lasts[0], LANES - HALF + 1, 1)),
-        prepare,
+        None,
         (lower_done_ref, upper_done_ref),
     )
     leaving_ref[...] = rows_after(upper_ref)

time: 33.1 us -> 33.1 us (level)
  no operation moved by 1% of the time
where the time goes in v9:
time: 33.1 us; the launch traced here: 32.6 us
  starting transfers between devices  19.4 us (59%)
  Pallas kernels  7.82 us (24%)
  waiting for transfers between devices  2.67 us (8%)
  local copies, waits for them, and re-layouts  2.64 us (8%)
    all_to_all x1, starting transfers between devices, local(): vectors = lax.all_to_all(pack(reflectors), 'col', 0, 0, tiled=True)  10.4 us
    ppermute x2, starting transfers between devices, neighbour(): lax.ppermute(value, 'row', [(i, i + step) for i in owners if i + step in...  9.01 us
    pallas_call x1, Pallas kernels, leave(): pl.pallas_call(leave_kernel, out_shape=tuple((jax.ShapeDtypeStruct(shape,...  2.82 us
    ppermute x2, waiting for transfers between devices, neighbour(): lax.ppermute(value, 'row', [(i, i + step) for i in owners if i + step in...  2.67 us
    unnamed x4, local copies, waits for them, and re-layouts  1.94 us
    pallas_call x1, Pallas kernels, upper(): pl.pallas_call(upper_kernel, out_shape=tuple((jax.ShapeDtypeStruct(shape,...  1.59 us
    pallas_call x1, Pallas kernels, lower(): pl.pallas_call(lower_kernel, out_shape=jax.ShapeDtypeStruct(OUT, jnp.floa...  1.22 us
    pallas_call x1, Pallas kernels, pack(): pl.pallas_call(pack_kernel, out_shape=jax.ShapeDtypeStruct((SWEEPS, 16, L...  0.94 us
  transfers between devices with their start and end apart: 3, of which 1 were waited for; matrix products, arithmetic and copies ran while one was open for 2% of the time, Pallas kernels for 9%

profile of v9, /device:TPU:6, one launch (start us, length us, event | category | flops | bytes accessed | tf_op | source)
XLA Modules:
  0.0 32.6 jit_solution(10586254092852453394)
XLA Ops:
  0.0 0.0 copy-start.1
  0.0 0.7 %copy-done.1 = f32[1,32,64]{2,1,0:T(8,128)S(1)} copy-done((f32[1,32,64]{2,1,0:T(8,128)S(1)}, f32[1,32,64]{2,1,0:T(8,128)}, u32[]{:S(2)}) %copy-start.1) | copy-done | bytes 8216
  0.7 0.9 %pack.1 = f32[16,16,128]{2,1,0:T(8,128)} custom-call(f32[1,32,64]{2,1,0:T(8,128)S(1)} %copy-done.1), custom_call_target="tpu_custom_call" | custom-call | tf_op jit(solution)/shard_map/pack/pallas_call | solution.py:50
  1.7 10.4 %all-to-all-start = ((f32[16,16,128]{2,1,0:T(8,128)}), f32[16,16,128]{2,1,0:T(8,128)S(1)}, u32[]{:S(2)}, u32[]{:S(2)}) async-start(f32[16,16,128]{2,1,0:T(8,128)} %pack.1), calls=%async_computation | async-start | bytes 262144 | tf_op jit(solution)/shard_map/all_to_all | solution.py:339
  12.1 0.7 %slice.3 = f32[16,128]{1,0:T(8,128)S(1)} slice(f32[2048,128]{1,0:T(8,128)} %rows_ref.1), slice={[0:16], [0:128]} | slice | bytes 16384 | tf_op jit(solution)/shard_map/slice | solution.py:340
  12.8 5.6 %collective-permute-start = (f32[16,128]{1,0:T(8,128)S(1)}, f32[16,128]{1,0:T(8,128)S(1)}, u32[]{:S(2)}, u32[]{:S(2)}) collective-permute-start(f32[16,128]{1,0:T(8,128)S(1)} %slice.3), channel_id=1, source_target_pairs={{16,0},{32,16},{48,32},{64,48},{80,64},{96,80},{112,96},{128,112},... | collective-permute-start | bytes 24584 | tf_op jit(solution)/shard_map/ppermute | solution.py:335
  18.4 0.0 copy-start
  18.4 1.2 %copy-done = f32[2048,128]{1,0:T(8,128)S(1)} copy-done((f32[2048,128]{1,0:T(8,128)S(1)}, f32[2048,128]{1,0:T(8,128)}, u32[]{:S(2)}) %copy-start) | copy-done | bytes 1048600
  19.7 0.9 %turn.1.tiles_ref = f32[2,64,16,128]{3,2,1,0:T(8,128)S(1)} custom-call(f32[2048,128]{1,0:T(8,128)S(1)} %copy-done), custom_call_target="tpu_custom_call" | custom-call | tf_op jit(solution)/shard_map/turn/pallas_call | solution.py:73
  20.6 0.0 collective-permute-done.halo_ref
  20.6 0.3 after.1
  20.9 0.0 all-to-all-done.vectors_ref
  20.9 2.8 %leave.1 = (f32[16,128]{1,0:T(8,128)S(1)}, f32[64,16,128]{2,1,0:T(8,128)S(1)}, f32[64,16,128]{2,1,0:T(8,128)S(1)}, f32[16,64,128]{2,1,0:T(8,128)S(1)}) custom-call(f32[2,64,16,128]{3,2,1,0:T(8,128)S(1)} %turn.1.tiles_ref, f32[16,16,128]{2,1,0:T(8,128)S(1)} %all-to-all-done.vectors_ref, f32[2,15,16,128]{3,2,1,0:T(8,128)S(1)} %get-tuple-element.14.after_ref), custom_call_target="tpu_custom_call" | custom-call | tf_op jit(solution)/shard_map/leave/pallas_call | solution.py:234
  23.8 3.4 %collective-permute-start.1 = (f32[16,128]{1,0:T(8,128)S(1)}, f32[16,128]{1,0:T(8,128)S(1)}, u32[]{:S(2)}, u32[]{:S(2)}) collective-permute-start(f32[16,128]{1,0:T(8,128)S(1)} %get-tuple-element.20), channel_id=1, source_target_pairs={{0,16},{16,32},{32,48},{48,64},{64,80},{80,96},{96,112},{112,128},... | collective-permute-start | bytes 24584 | tf_op jit(solution)/shard_map/ppermute | solution.py:335
  27.1 1.6 %upper.1 = (f32[32,64,128]{2,1,0:T(8,128)}, f32[8,128,128]{2,1,0:T(8,128)S(1)}, f32[8,16,128]{2,1,0:T(8,128)S(1)}) custom-call(f32[64,16,128]{2,1,0:T(8,128)S(1)} %get-tuple-element.15.lower_ref, f32[64,16,128]{2,1,0:T(8,128)S(1)} %get-tuple-element.16.upper_ref, f32[16,64,128]{2,1,0:T(8,128)S(1)} %get-tuple-element.17.spread_ref), custom_call_target="tpu_custom_call" | custom-call | tf_op jit(solution)/shard_map/upper/pallas_call | solution.py:282
  28.8 2.7 %collective-permute-done.1.entering_ref = f32[16,128]{1,0:T(8,128)S(1)} collective-permute-done((f32[16,128]{1,0:T(8,128)S(1)}, f32[16,128]{1,0:T(8,128)S(1)}, u32[]{:S(2)}, u32[]{:S(2)}) %collective-permute-start.1) | collective-permute-done | bytes 8224 | tf_op jit(solution)/shard_map/ppermute | solution.py:335
  31.4 1.2 %lower.1 = f32[32,64,128]{2,1,0:T(8,128)} custom-call(f32[8,128,128]{2,1,0:T(8,128)S(1)} %get-tuple-element.18.fixed_ref, f32[8,16,128]{2,1,0:T(8,128)S(1)} %get-tuple-element.19.response_ref, f32[16,128]{1,0:T(8,128)S(1)} %collective-permute-done.1.entering_ref, f32[16,128]{1,0:T(8,128)S(1)} %get-tuple-element.21.own_ref, ...), custom_call_target="tpu_custom_call", output_to_operand_aliasing={{}: (4, {})} | custom-call | tf_op jit(solution)/shard_map/lower/pallas_call | solution.py:321
Async XLA Ops:
  0.0 0.7 %copy-start.1 = (f32[1,32,64]{2,1,0:T(8,128)S(1)}, f32[1,32,64]{2,1,0:T(8,128)}, u32[]{:S(2)}) copy-start(f32[1,32,64]{2,1,0:T(8,128)} %reflectors_ref.1) | copy-start | bytes 24580
  1.7 19.3 %all-to-all-start = ((f32[16,16,128]{2,1,0:T(8,128)}), f32[16,16,128]{2,1,0:T(8,128)S(1)}, u32[]{:S(2)}, u32[]{:S(2)}) async-start(f32[16,16,128]{2,1,0:T(8,128)} %pack.1), calls=%async_computation | async-start | bytes 262144 | tf_op jit(solution)/shard_map/all_to_all | solution.py:339
  12.8 7.8 %collective-permute-start = (f32[16,128]{1,0:T(8,128)S(1)}, f32[16,128]{1,0:T(8,128)S(1)}, u32[]{:S(2)}, u32[]{:S(2)}) collective-permute-start(f32[16,128]{1,0:T(8,128)S(1)} %slice.3), channel_id=1, source_target_pairs={{16,0},{32,16},{48,32},{64,48},{80,64},{96,80},{112,96},{128,112},... | collective-permute-start | bytes 24584 | tf_op jit(solution)/shard_map/ppermute | solution.py:335
  18.4 1.2 %copy-start = (f32[2048,128]{1,0:T(8,128)S(1)}, f32[2048,128]{1,0:T(8,128)}, u32[]{:S(2)}) copy-start(f32[2048,128]{1,0:T(8,128)} %rows_ref.1) | copy-start | bytes 3145732
  23.8 7.7 %collective-permute-start.1 = (f32[16,128]{1,0:T(8,128)S(1)}, f32[16,128]{1,0:T(8,128)S(1)}, u32[]{:S(2)}, u32[]{:S(2)}) collective-permute-start(f32[16,128]{1,0:T(8,128)S(1)} %get-tuple-element.20), channel_id=1, source_target_pairs={{0,16},{16,32},{32,48},{48,64},{64,80},{80,96},{96,112},{112,128},... | collective-permute-start | bytes 24584 | tf_op jit(solution)/shard_map/ppermute | solution.py:335
